TPU v7x, 128 devices: a whole 4x4x4 slice. The times are simulated.
128 devices in a mesh: blk: 8 (over z, x_lo), dp: 16 (over x_hi, y, core).
Axes of the slice: x: 4 (x_hi: 2, x_lo: 2; x = x_hi * 2 + x_lo), y: 4, z: 4, core: 2. Of those that a mesh axis runs over, the one named last changes fastest.
Arguments:
- queries: bfloat16 [16, 8192, 2560], P('dp', 'blk'), may hold values from -16 to 16, as said below
- candidates: bfloat16 [16, 1024, 2560], P('dp', 'blk'), may hold values from -6 to 6, as said below
- loss_weight: float32 [16, 8192], P('dp', 'blk'), may hold values from 8 to 80
- positives: int32 [16, 8192], P('dp', 'blk'), may hold values from 0 to 1023
- producers: int32 [16, 1024, 1], P('dp', 'blk'), may hold values from 0 to 127; in each aligned block of 128 rows (0 to 127, 128 to 255, ..., all dimensions but the last counted through in order) at most 4 rows name the same one
- rows: int32 [16, 1024], P('dp', 'blk'), may hold values from 0 to 255
Outputs:
- query_grad: bfloat16 [16, 8192, 2560], P('dp', 'blk')
- decoder_grad: float32 [32768, 2560], P(('blk', 'dp'))
Inputs may be any that keep to these rules, and one draw needn't show every extreme that they name: `producers`: decoder shard s is the device with blk index s // (number of dp devices) and dp index s % (number of dp devices). Among the 128 hypotheses on one device no decoder shard appears more than 4 times, and in every draw some device has a shard that appears exactly 4 times. `queries`: Real-valued embeddings. `candidates`: Real-valued embeddings.
All inputs are finite; a program needn't handle non-finite values.
Results may differ from a plain program's by a relative error of at most 0.005.
Values may be sent and summed in bfloat16 or wider, within the bound.
A program may use at most 128 MiB of HBM per device.

v0:
```python
import math

import jax
import jax.numpy as jnp
from jax import lax
from jax.sharding import PartitionSpec as P

D = 2560
HR = 256
MOST = 4


def coefficients(scores, weight, target):
    row_max = jnp.max(scores, axis=1, keepdims=True)
    shifted = jnp.exp(scores - row_max)
    chance = shifted / jnp.sum(shifted, axis=1, keepdims=True)
    column_ids = jnp.arange(scores.shape[1], dtype=jnp.int32)
    onehot = (column_ids[None, :] == target[:, None]).astype(jnp.float32)
    return (weight[:, None] * (chance - onehot)).astype(jnp.bfloat16)


def per_device(queries, candidates, loss_weight, positives, producers, rows):
    scale_factor = 1.0 / math.sqrt(D)
    query_rows = queries[0]
    own_rows = candidates[0]
    weight = loss_weight[0]
    target = positives[0]
    all_rows = lax.all_gather(own_rows, "blk", axis=0, tiled=True)
    scores = jnp.dot(query_rows, all_rows.T, preferred_element_type=jnp.float32) * scale_factor
    coefficient = coefficients(scores, weight, target)
    query_total = jnp.dot(coefficient, all_rows, preferred_element_type=jnp.float32)
    query_grad = (query_total * scale_factor).astype(jnp.bfloat16)[None]
    product = lax.dot_general(
        coefficient, query_rows, (((0,), (0,)), ((), ())), preferred_element_type=jnp.float32
    )
    cand_grad = lax.psum_scatter(product * scale_factor, "blk", scatter_dimension=0, tiled=True)
    shards = lax.axis_size("blk") * lax.axis_size("dp")
    hyp_count = cand_grad.shape[0]
    target_shard = producers[0, :, 0]
    decoder_row = rows[0]
    member = (target_shard[:, None] == jnp.arange(shards, dtype=jnp.int32)[None, :]).astype(
        jnp.int32
    )
    position = jnp.sum(jnp.cumsum(member, axis=0) * member, axis=1) - 1
    slot_index = target_shard * MOST + position
    inverse = (
        jnp.full((shards * MOST,), hyp_count, jnp.int32)
        .at[slot_index]
        .set(jnp.arange(hyp_count, dtype=jnp.int32))
    )
    padded_grad = jnp.concatenate(
        [cand_grad, jnp.zeros((1, cand_grad.shape[1]), jnp.float32)], axis=0
    )
    buffer = jnp.take(padded_grad, inverse, axis=0)
    slot_rows = jnp.full((shards * MOST,), -1, jnp.int32).at[slot_index].set(decoder_row)
    arrived, arrived_rows = (
        lax.all_to_all(buffer, ("blk", "dp"), split_axis=0, concat_axis=0, tiled=True),
        lax.all_to_all(slot_rows, ("blk", "dp"), split_axis=0, concat_axis=0, tiled=True),
    )
    landing = jnp.where(arrived_rows < 0, HR, arrived_rows)
    decoder_grad = (
        jnp.zeros((HR, arrived.shape[1]), jnp.float32).at[landing].add(arrived, mode="drop")
    )
    return (query_grad, decoder_grad)


def solution(mesh):
    return jax.shard_map(
        per_device,
        mesh=mesh,
        in_specs=(
            P("dp", "blk", None),
            P("dp", "blk", None),
            P("dp", "blk"),
            P("dp", "blk"),
            P("dp", "blk", None),
            P("dp", "blk"),
        ),
        out_specs=(P("dp", "blk", None), P(("blk", "dp"), None)),
        check_vma=False,
    )
```

profile of v0, /device:TPU:0, one launch (start us, length us, event | category | flops | bytes accessed | tf_op | source)
XLA Modules:
  0.0 469.6 jit_solution(13905703907354258618)
XLA Ops:
  7.2 0.0 all-gather.3.cloned.1.call-start
  7.2 0.7 all-gather.3.cloned.1.call-update
  7.9 0.0 reduce-scatter.2.cloned.1.call-start
  7.9 114.4 %all-gather.3.cloned.1.call-done = bf16[1,1024,2560]{2,1,0:T(8,128)(2,1)} async-done(((bf16[1,128,2560]{2,1,0:T(8,128)(2,1)}), bf16[1,1024,2560]{2,1,0:T(8,128)(2,1)}) %all-gather.3.cloned.1.call-update) | async-done | bytes 5242896 | tf_op jit(solution)/shard_map/all_gather | solution.py:28
  122.4 9.6 %multiply_reduce_fusion = (f32[1024]{0:T(1024)S(1)}, f32[1024,1024]{0,1:T(8,128)S(1)}) fusion(bf16[1,1024,2560]{2,1,0:T(8,128)(2,1)} %all-gather.3.cloned.1.call-done, bf16[1,1024,2560]{2,1,0:T(8,128)(2,1)} %param.6), kind=kOutput, calls=%fused_computation.15 | convolution fusion | flops 5370805248 | bytes 14684160 | tf_op jit(solution)/shard_map/dot_general | solution.py:29
  132.0 0.0 copy-start.3
  132.0 0.7 fusion.8
  132.8 1.2 copy-done
  134.0 8.5 %convolution_multiply_fusion = f32[1024,2560]{1,0:T(8,128)} fusion(bf16[1,1024,2560]{2,1,0:T(8,128)(2,1)S(1)} %copy-done.2, f32[1024,1024]{0,1:T(8,128)S(1)} %get-tuple-element.3, s32[1024]{0:T(1024)S(1)} %bitcast.36, f32[1024]{0:T(1024)S(1)} %fusion.8, f32[1024]{0:T(1024)S(1)} %get-tuple-element.2, f32[1024]{0:T(1024)S(1)} %bitcast.38), kind=kOutput, calls=%fused_computation.5 | convolution fusion | flops 5379719168 | bytes 19939328 | tf_op jit(solution)/shard_map/dot_general | solution.py:33
  142.5 0.0 reduce-scatter.2.cloned.1.call-update
  142.5 0.6 copy-done.1
  143.2 0.1 fusion.11
  143.2 0.2 reduce_window_sum.11
  143.4 0.2 select_reduce_fusion
  143.6 1.1 scatter_custom_fusion
  144.7 0.7 all_to_all.14
  145.5 8.9 %all-to-all-start = ((s32[128,4,1]{1,2,0:T(1,128)}), s32[128,4,1]{1,2,0:T(1,128)S(1)}, u32[]{:S(2)}, u32[]{:S(2)}) async-start(s32[128,4,1]{1,2,0:T(1,128)} %bitcast.10), calls=%async_computation | async-start | bytes 131072 | tf_op jit(solution)/shard_map/all_to_all | solution.py:58
  154.3 1.0 scatter_custom_fusion.1
  155.3 0.1 broadcast_in_dim.43
  155.5 196.7 %reduce-scatter.2.cloned.1.call-done = f32[128,2560]{1,0:T(8,128)} async-done(((f32[1024,2560]{1,0:T(8,128)}), f32[128,2560]{1,0:T(8,128)}) %reduce-scatter.2.cloned.1.call-update) | async-done | bytes 1310736 | tf_op jit(solution)/shard_map/reduce_scatter | solution.py:36
  352.1 1.4 concatenate.3
  353.6 4.1 gather_fusion
  357.7 7.1 %gather.7 = f32[128,4,2560]{2,1,0:T(4,128)} reshape(f32[512,2560]{1,0:T(8,128)} %gather_fusion) | data formatting | bytes 10485760 | tf_op jit(solution)/shard_map/jit(_take)/gather | solution.py:54
  364.8 6.0 %broadcast_select_fusion = f32[128,4,2560]{2,1,0:T(4,128)} fusion(f32[128,4,2560]{2,1,0:T(4,128)} %gather.7, pred[128,4]{1,0:T(8,128)(4,1)S(1)} %broadcast_in_dim.43), kind=kLoop, calls=%fused_computation.17 | loop fusion | flops 1310720 | bytes 10486272 | tf_op jit(solution)/shard_map/jit(_take)/select_n | solution.py:54
  370.9 10.4 %all-to-all-start.1 = ((f32[128,4,2560]{2,1,0:T(4,128)}), f32[128,4,2560]{2,1,0:T(4,128)}, u32[]{:S(2)}, u32[]{:S(2)}) async-start(f32[128,4,2560]{2,1,0:T(4,128)} %broadcast_select_fusion), calls=%async_computation.2 | async-start | bytes 10485760 | tf_op jit(solution)/shard_map/all_to_all | solution.py:57
  381.3 0.5 broadcast.116
  381.8 0.8 reduce.3
  382.6 0.1 all_to_all.16
  382.7 10.8 %fusion.5 = bf16[1,1024,2560]{2,1,0:T(8,128)(2,1)} fusion(bf16[1,1024,2560]{2,1,0:T(8,128)(2,1)} %all-gather.3.cloned.1.call-done, f32[1024,1024]{0,1:T(8,128)} %copy-done, s32[1024]{0:T(1024)S(1)} %bitcast.37, f32[1024]{0:T(1024)S(1)} %fusion.8, f32[1024]{0:T(1024)S(1)} %get-tuple-element.2, f32[1024]{0:T(1024)S(1)} %bitcast.39), kind=kOutput, calls=%fused_computation.11 | convolution fusion | flops 5382340608 | bytes 14696448 | tf_op jit(solution)/shard_map/dot_general | solution.py:31
  393.5 50.6 %all-to-all-done.1 = f32[128,4,2560]{2,1,0:T(4,128)} async-done(((f32[128,4,2560]{2,1,0:T(4,128)}), f32[128,4,2560]{2,1,0:T(4,128)}, u32[]{:S(2)}, u32[]{:S(2)}) %all-to-all-start.1) | async-done | bytes 5242912 | tf_op jit(solution)/shard_map/all_to_all | solution.py:57
  444.1 7.2 %reshape.113 = f32[512,2560]{1,0:T(8,128)} reshape(f32[128,4,2560]{2,1,0:T(4,128)} %all-to-all-done.1) | data formatting | bytes 10485760 | tf_op jit(solution)/shard_map/all_to_all | solution.py:57
  451.3 11.4 %scatter_custom_fusion.2 = f32[256,2560]{1,0:T(8,128)} fusion(s32[512]{0:T(512)S(1)} %bitcast.35, f32[512,2560]{1,0:T(8,128)} %reshape.113, f32[]{:T(128)} %constant.13.clone.1), kind=kCustom, calls=%fused_computation.18 | custom fusion | flops 1310720 | bytes 2621952 | tf_op jit(solution)/shard_map/scatter-add | solution.py:62
  (14 shorter events, 0.1 us)
Async XLA Ops:
  7.2 115.2 %all-gather.3.cloned.1.call-start = ((), (), s32[]{:S(2)}) async-start(), calls=%async_computation.4 | async-start | bytes 5898240 | tf_op jit(solution)/shard_map/all_gather | solution.py:28
  7.9 344.3 %reduce-scatter.2.cloned.1.call-start = ((), (), s32[]{:S(2)}) async-start(), calls=%async_computation.3 | async-start | bytes 11796480 | tf_op jit(solution)/shard_map/reduce_scatter | solution.py:36
  122.4 11.6 %copy-start.2 = (bf16[1,1024,2560]{2,1,0:T(8,128)(2,1)S(1)}, bf16[1,1024,2560]{2,1,0:T(8,128)(2,1)}, u32[]{:S(2)}) copy-start(bf16[1,1024,2560]{2,1,0:T(8,128)(2,1)} %param.6) | copy-start | bytes 15728644
  132.0 2.0 copy-start
  132.0 2.0 copy-start.3
  132.0 2.0 copy-start.4
  142.5 0.7 copy-start.1
  145.5 225.4 %all-to-all-start = ((s32[128,4,1]{1,2,0:T(1,128)}), s32[128,4,1]{1,2,0:T(1,128)S(1)}, u32[]{:S(2)}, u32[]{:S(2)}) async-start(s32[128,4,1]{1,2,0:T(1,128)} %bitcast.10), calls=%async_computation | async-start | bytes 131072 | tf_op jit(solution)/shard_map/all_to_all | solution.py:58
  370.9 73.2 %all-to-all-start.1 = ((f32[128,4,2560]{2,1,0:T(4,128)}), f32[128,4,2560]{2,1,0:T(4,128)}, u32[]{:S(2)}, u32[]{:S(2)}) async-start(f32[128,4,2560]{2,1,0:T(4,128)} %broadcast_select_fusion), calls=%async_computation.2 | async-start | bytes 10485760 | tf_op jit(solution)/shard_map/all_to_all | solution.py:57
Sparse Core Ops, SparseCore 0:
  9.6 112.6 all-gather.2
  142.6 209.4 reduce-scatter.1
where the time goes:
time: 472 us; the launch traced here: 470 us
  waiting for transfers between devices  362 us (77%)
  matrix products  28.9 us (6%)
  local copies, waits for them, and re-layouts  25.3 us (5%)
  other arithmetic  19.5 us (4%)
  starting transfers between devices  19.4 us (4%)
  between operations  14.2 us (3%)
    reduce_scatter x1, waiting for transfers between devices, per_device(): lax.psum_scatter(product * scale_factor, 'blk', scatter_dimension=0, tile...  197 us
    all_gather x1, waiting for transfers between devices, per_device(): all_rows = lax.all_gather(own_rows, 'blk', axis=0, tiled=True)  114 us
    all_to_all x1, waiting for transfers between devices, per_device(): lax.all_to_all(buffer, ('blk', 'dp'), split_axis=0, concat_axis=0, tiled=...  50.6 us
    scatter-add x1, other arithmetic, per_device(): jnp.zeros((HR, arrived.shape[1]), jnp.float32).at[landing]  11.4 us
    gather x2, local copies, waits for them, and re-layouts, per_device(): buffer = jnp.take(padded_grad, inverse, axis=0)  11.2 us
    dot_general x1, matrix products, per_device(): jnp.dot(coefficient, all_rows, preferred_element_type=jnp.float32)  10.8 us
    all_to_all x1, starting transfers between devices, per_device(): lax.all_to_all(buffer, ('blk', 'dp'), split_axis=0, concat_axis=0, tiled=...  10.4 us
    dot_general x1, matrix products, per_device(): jnp.dot(query_rows, all_rows.T, preferred_element_type=jnp.float32)  9.61 us
  transfers between devices with their start and end apart: 4, of which 3 were waited for; matrix products, arithmetic and copies ran while one was open for 7% of the time, Pallas kernels for 0%

commit v1 on v0

v1 whole, which is shorter than its diff:
```python
import functools
import math

import jax
import jax.numpy as jnp
from jax import lax
from jax.experimental import pallas as pl
from jax.experimental.pallas import tpu as pltpu
from jax.sharding import PartitionSpec as P

D = 2560
HR = 256
MOST = 4
NQ = 1024
CB = 128
HB = 64
NC = 5
CW = D // NC
SHARDS = 128
SCALE = 1.0 / math.sqrt(D)
F32, BF16, I32 = jnp.float32, jnp.bfloat16, jnp.int32

SELF, XN, ZP, ZM, Z2 = 0, 2, 4, 6, 8
ZPX, ZMX, Z2X = (10, 13), (11, 14), (12, 15)
GROUPS = ((0, 4), (4, 4), (8, 5), (13, 3))

MESSAGES = (
    (0, 2, "x"), (2, 2, "p"), (4, 2, "m"), (6, 1, "p"), (7, 1, "m"),
    (8, 1, "p"), (9, 1, "m"), (10, 2, "x"), (12, 1, "p"), (13, 1, "m"),
)
NM = len(MESSAGES)


def main_kernel(
    q_hbm, c_hbm, w_ref, pos_ref, trow_ref, tcol_ref, qg_hbm, slots_ref,
    q, c, e, coef_t, coef, prod, snd, rcv, qg, sel, gs, mx, sm,
    q_sem, c_sem, ag_send, ag_recv, rs_send, rs_recv, qg_sem,
):
    blk = lax.axis_index("blk")
    z, x = blk // 2, blk % 2

    def at(dz, dx):
        return ((z + dz) % 4) * 2 + (x + dx) % 2

    peers = {"x": at(0, 1), "p": at(1, 0), "m": at(3, 0)}

    q_copy = pltpu.make_async_copy(q_hbm.at[0], q, q_sem)
    q_copy.start()
    own = [
        pltpu.make_async_copy(c_hbm.at[0, pl.ds(h * HB, HB)], c.at[h], c_sem.at[h]) for h in (0, 1)
    ]
    for copy in own:
        copy.start()

    barrier = pltpu.get_barrier_semaphore()
    for peer in peers.values():
        pl.semaphore_signal(
            barrier, inc=1, device_id={"blk": peer}, device_id_type=pl.DeviceIdType.MESH
        )
    pl.semaphore_wait(barrier, 3)

    def ag(src, dst, way):
        source = c_hbm.at[0, pl.ds(src * HB, HB)] if src < 2 else c.at[src]
        return pltpu.make_async_remote_copy(
            src_ref=source,
            dst_ref=c.at[dst],
            send_sem=ag_send.at[dst],
            recv_sem=ag_recv.at[dst],
            device_id={"blk": peers[way]},
            device_id_type=pl.DeviceIdType.MESH,
        )

    gather = {
        ZM: ag(0, ZM, "p"), ZP + 1: ag(1, ZP + 1, "m"), XN: ag(0, XN, "x"),
        ZM + 1: ag(1, ZM + 1, "p"), ZP: ag(0, ZP, "m"), XN + 1: ag(1, XN + 1, "x"),
        Z2: ag(ZM, Z2, "p"), Z2 + 1: ag(ZP + 1, Z2 + 1, "m"),
        ZMX[0]: ag(XN, ZMX[0], "p"), ZPX[0]: ag(XN, ZPX[0], "m"),
        ZMX[1]: ag(XN + 1, ZMX[1], "p"), ZPX[1]: ag(XN + 1, ZPX[1], "m"),
        Z2X[0]: ag(Z2, Z2X[0], "x"), Z2X[1]: ag(Z2 + 1, Z2X[1], "x"),
    }
    for slot in (ZM, ZP + 1, XN, ZM + 1, ZP, XN + 1):
        gather[slot].start()

    earlier = (tcol_ref[...] == trow_ref[...]) & (
        lax.broadcasted_iota(I32, (CB, CB), 0) < lax.broadcasted_iota(I32, (CB, CB), 1)
    )
    place = jnp.sum(earlier.astype(I32), axis=0, keepdims=True)
    slot_index = trow_ref[...] * MOST + place
    keys = jnp.concatenate([slot_index * 4 + part for part in range(4)], axis=1)

    def fill(i, _):
        row = i * 256 + lax.broadcasted_iota(I32, (256, 4 * CB), 0)
        key = ((row // 16) * MOST + row % 4) * 4 + (row // 4) % 4
        sel[pl.ds(pl.multiple_of(i * 256, 256), 256), :] = (key == keys).astype(F32).astype(BF16)
        return 0

    lax.fori_loop(0, 16 * SHARDS // 256, fill, 0)
    q_copy.wait()
    for copy in own:
        copy.wait()

    def scores(which):
        first, number = GROUPS[which]

        def part(i, _):
            span = pl.ds(pl.multiple_of(i * 256, 256), 256)
            s = lax.dot_general(
                c[first : first + number].reshape(number * HB, D), q[span, :],
                (((1,), (1,)), ((), ())), preferred_element_type=F32,
            ) * SCALE
            top = jnp.max(s, axis=0, keepdims=True)
            shifted = jnp.exp(s - top)
            e[first : first + number, :, span] = shifted.reshape(number, HB, 256)
            mx[which : which + 1, span] = top
            sm[which : which + 1, span] = jnp.sum(shifted, axis=0, keepdims=True)
            return 0

        lax.fori_loop(0, NQ // 256, part, 0)

    gather[ZM].wait_recv()
    gather[Z2].start()
    gather[ZP + 1].wait_recv()
    gather[Z2 + 1].start()
    gather[XN].wait_recv()
    gather[XN + 1].wait_recv()
    scores(0)
    gather[ZM + 1].wait_recv()
    gather[ZP].wait_recv()
    scores(1)
    gather[Z2].wait_recv()
    gather[Z2X[0]].start()
    gather[Z2 + 1].wait_recv()
    gather[Z2X[1]].start()
    for slot in (ZMX[0], ZPX[0], ZMX[1], ZPX[1]):
        gather[slot].start()
    for slot in (ZPX[0], ZMX[0], Z2X[0]):
        gather[slot].wait_recv()
    scores(2)
    for slot in (ZPX[1], ZMX[1], Z2X[1]):
        gather[slot].wait_recv()
    scores(3)

    top = jnp.max(mx[0:4], axis=0, keepdims=True)
    rescale = jnp.exp(mx[0:4] - top)
    inverse = 1.0 / jnp.sum(rescale * sm[0:4], axis=0, keepdims=True)
    weight, target = w_ref[...], pos_ref[...]
    places = {
        0: at(0, 0), 2: at(0, 1), 4: at(1, 0), 6: at(3, 0), 8: at(2, 0),
    }
    starts = [0] * 16
    for first, owner in places.items():
        starts[first], starts[first + 1] = owner * CB, owner * CB + HB
    for (low, high), owner in ((ZPX, at(1, 1)), (ZMX, at(3, 1)), (Z2X, at(2, 1))):
        starts[low], starts[high] = owner * CB, owner * CB + HB
    for which, (first, number) in enumerate(GROUPS):
        factor = rescale[which : which + 1] * inverse
        for k in range(first, first + number):
            ids = starts[k] + lax.broadcasted_iota(I32, (HB, NQ), 0)
            onehot = (ids == target).astype(F32)
            coef_t[k] = (weight * (e[k] * factor - onehot)).astype(BF16)

    def message(m, chunk):
        first, number, way = MESSAGES[m]
        return pltpu.make_async_remote_copy(
            src_ref=snd.at[chunk, pl.ds(first, number)],
            dst_ref=rcv.at[chunk, pl.ds(first, number)],
            send_sem=rs_send.at[chunk, m],
            recv_sem=rs_recv.at[chunk, m],
            device_id={"blk": peers[way]},
            device_id_type=pl.DeviceIdType.MESH,
        )

    def qg_copy(chunk):
        return pltpu.make_async_copy(
            qg.at[chunk],
            qg_hbm.at[0, :, pl.ds(pl.multiple_of(chunk * CW, CW), CW)],
            qg_sem.at[chunk],
        )

    def put(chunk, slot, value):
        snd[chunk, slot] = value.astype(BF16)

    def got(chunk, slot):
        return rcv[chunk, slot].astype(F32)

    def step(i, _):
        @pl.when(i < NC)
        def _():
            for half in range(CW // 256):
                columns = pl.ds(pl.multiple_of(i * CW + half * 256, 256), 256)
                block = jnp.dot(
                    coef_t[...].reshape(16 * HB, NQ), q[:, columns], preferred_element_type=F32
                ) * SCALE
                prod[i, :, :, half * 256 : half * 256 + 256] = block.reshape(16, HB, 256)
            put(i, 0, prod[i, Z2X[0]])
            put(i, 1, prod[i, Z2X[1]])
            message(0, i).start()
            put(i, 2, prod[i, ZPX[0]])
            put(i, 3, prod[i, ZPX[1]])
            message(1, i).start()
            put(i, 4, prod[i, ZMX[0]])
            put(i, 5, prod[i, ZMX[1]])
            message(2, i).start()
            put(i, 6, prod[i, ZP])
            message(3, i).start()
            put(i, 7, prod[i, ZM + 1])
            message(4, i).start()

        @pl.when(i == 0)
        def _():
            for k in range(4):
                coef[pl.ds(k * 256, 256), :] = jnp.transpose(
                    coef_t[:, :, k * 256 : k * 256 + 256].reshape(16 * HB, 256)
                )

        @pl.when(i < NC)
        def _():
            for half in range(CW // 256):
                columns = pl.ds(pl.multiple_of(i * CW + half * 256, 256), 256)
                total = jnp.dot(
                    coef[...], c[:, :, columns].reshape(16 * HB, 256), preferred_element_type=F32
                )
                qg[i, :, half * 256 : half * 256 + 256] = (total * SCALE).astype(BF16)
            qg_copy(i).start()

        @pl.when((i >= 1) & (i <= NC))
        def _():
            k = i - 1
            message(0, k).wait_recv()
            put(k, 9, prod[k, Z2] + got(k, 0))
            message(6, k).start()
            put(k, 8, prod[k, Z2 + 1] + got(k, 1))
            message(5, k).start()
            message(1, k).wait_recv()
            message(2, k).wait_recv()
            put(k, 10, prod[k, XN] + got(k, 2) + got(k, 4))
            put(k, 11, prod[k, XN + 1] + got(k, 3) + got(k, 5))
            message(7, k).start()

        @pl.when((i >= 2) & (i <= NC + 1))
        def _():
            k = i - 2
            message(5, k).wait_recv()
            put(k, 12, prod[k, ZP + 1] + got(k, 8))
            message(8, k).start()
            message(6, k).wait_recv()
            put(k, 13, prod[k, ZM] + got(k, 9))
            message(9, k).start()

        @pl.when(i >= 3)
        def _():
            k = i - 3
            for m in (3, 4, 7, 8, 9):
                message(m, k).wait_recv()
            low = prod[k, SELF] + got(k, 6) + got(k, 13) + got(k, 10)
            high = prod[k, SELF + 1] + got(k, 7) + got(k, 12) + got(k, 11)
            for part in range(4):
                gs[part * CB : part * CB + HB, :] = low[:, part * 128 : part * 128 + 128].astype(BF16)
                gs[part * CB + HB : part * CB + CB, :] = high[
                    :, part * 128 : part * 128 + 128
                ].astype(BF16)
            picked = jnp.dot(sel[...], gs[...], preferred_element_type=F32)
            slots_ref[:, :, pl.ds(pl.multiple_of(k * 128, 128), 128)] = picked.astype(BF16).reshape(
                SHARDS, 16, 128
            )

        return 0

    lax.fori_loop(0, NC + 3, step, 0)

    for copy in gather.values():
        copy.wait_send()

    def drain(i, _):
        for m in range(NM):
            message(m, i).wait_send()
        qg_copy(i).wait()
        return 0

    lax.fori_loop(0, NC, drain, 0)


def key_kernel(me_ref, shard_ref, row_ref, key_ref):
    hits = (shard_ref[...] == me_ref[0]).astype(F32)
    before = (
        lax.broadcasted_iota(I32, (CB, CB), 0) < lax.broadcasted_iota(I32, (CB, CB), 1)
    ).astype(F32)
    place = jnp.dot(hits.astype(BF16), before.astype(BF16), preferred_element_type=F32)
    numbers = (row_ref[...] + 1).astype(F32) * hits
    lanes = lax.broadcasted_iota(I32, (SHARDS, 16 * SHARDS), 1)
    spread = (lanes // 16 == lax.broadcasted_iota(I32, (SHARDS, 16 * SHARDS), 0)).astype(F32)
    spread = spread.astype(BF16)
    slot = lax.broadcasted_iota(I32, (8, 16 * SHARDS), 1) % 4
    total = jnp.zeros((8, 16 * SHARDS), F32)
    for k in range(MOST):
        chosen = jnp.where(place == float(k), numbers, 0.0).astype(BF16)
        by_source = lax.dot_general(
            jnp.ones((8, CB), BF16), chosen, (((1,), (1,)), ((), ())), preferred_element_type=F32
        )
        wide = jnp.dot(by_source.astype(BF16), spread, preferred_element_type=F32)
        total = total + jnp.where(slot == k, wide, 0.0)
    key_ref[...] = total.astype(I32) - 1


def landing_kernel(key_ref, arrived_ref, out_ref, land):
    key = key_ref[0:1, :]
    part = (lax.broadcasted_iota(I32, (1, 16 * SHARDS), 1) // 4) % 4
    rows = lax.broadcasted_iota(I32, (HR, 16 * SHARDS), 0)
    for k in range(4):
        land[k * HR : k * HR + HR, :] = (rows == jnp.where(part == k, key, -1)).astype(F32).astype(BF16)
    for chunk in range(NC):
        total = jnp.dot(
            land[...],
            arrived_ref[:, :, chunk * 128 : chunk * 128 + 128].reshape(16 * SHARDS, 128),
            preferred_element_type=F32,
        )
        for k in range(4):
            first = chunk * CW + k * 128
            out_ref[:, first : first + 128] = total[k * HR : k * HR + HR]


def per_device(queries, candidates, loss_weight, positives, producers, rows):
    vmem, hbm = pl.BlockSpec(memory_space=pltpu.VMEM), pl.BlockSpec(memory_space=pl.ANY)
    shard_row = producers.reshape(1, CB)
    shard_column = producers.reshape(CB, 1)
    meta = lax.all_gather(
        jnp.concatenate([shard_row, rows], axis=0), ("blk", "dp"), axis=0, tiled=False
    )
    query_grad, slots = pl.pallas_call(
        main_kernel,
        out_shape=(
            jax.ShapeDtypeStruct((1, NQ, D), BF16),
            jax.ShapeDtypeStruct((SHARDS, 16, D // 4), BF16),
        ),
        in_specs=[hbm, hbm, vmem, vmem, vmem, vmem],
        out_specs=(hbm, vmem),
        scratch_shapes=[
            pltpu.VMEM((NQ, D), BF16),
            pltpu.VMEM((16, HB, D), BF16),
            pltpu.VMEM((16, HB, NQ), F32),
            pltpu.VMEM((16, HB, NQ), BF16),
            pltpu.VMEM((NQ, 16 * HB), BF16),
            pltpu.VMEM((NC, 16, HB, CW), F32),
            pltpu.VMEM((NC, 14, HB, CW), BF16),
            pltpu.VMEM((NC, 14, HB, CW), BF16),
            pltpu.VMEM((NC, NQ, CW), BF16),
            pltpu.VMEM((16 * SHARDS, 4 * CB), BF16),
            pltpu.VMEM((4 * CB, 128), BF16),
            pltpu.VMEM((8, NQ), F32),
            pltpu.VMEM((8, NQ), F32),
            pltpu.SemaphoreType.DMA,
            pltpu.SemaphoreType.DMA((2,)),
            pltpu.SemaphoreType.DMA((16,)),
            pltpu.SemaphoreType.DMA((16,)),
            pltpu.SemaphoreType.DMA((NC, NM)),
            pltpu.SemaphoreType.DMA((NC, NM)),
            pltpu.SemaphoreType.DMA((NC,)),
        ],
        compiler_params=pltpu.CompilerParams(
            collective_id=0, has_side_effects=True, vmem_limit_bytes=60 * 2**20
        ),
        cost_estimate=pl.CostEstimate(
            flops=6 * NQ * NQ * D, bytes_accessed=14 * 2**20, transcendentals=NQ * NQ
        ),
        name="gather_scores_reduce",
    )(queries, candidates, loss_weight, positives, shard_row, shard_column)
    arrived = lax.all_to_all(slots, ("blk", "dp"), split_axis=0, concat_axis=0, tiled=True)
    me = lax.axis_index("blk") * lax.axis_size("dp") + lax.axis_index("dp")
    key = pl.pallas_call(
        key_kernel,
        out_shape=jax.ShapeDtypeStruct((8, 16 * SHARDS), I32),
        in_specs=[pl.BlockSpec(memory_space=pltpu.SMEM), vmem, vmem],
        out_specs=vmem,
        name="slot_rows",
    )(me.astype(I32).reshape(1), meta[:, 0], meta[:, 1])
    decoder_grad = pl.pallas_call(
        landing_kernel,
        out_shape=jax.ShapeDtypeStruct((HR, D), F32),
        in_specs=[vmem, vmem],
        out_specs=vmem,
        scratch_shapes=[pltpu.VMEM((4 * HR, 16 * SHARDS), BF16)],
        compiler_params=pltpu.CompilerParams(vmem_limit_bytes=40 * 2**20),
        name="landing",
    )(key, arrived)
    return query_grad, decoder_grad


def solution(mesh):
    return jax.shard_map(
        per_device,
        mesh=mesh,
        in_specs=(
            P("dp", "blk", None),
            P("dp", "blk", None),
            P("dp", "blk"),
            P("dp", "blk"),
            P("dp", "blk", None),
            P("dp", "blk"),
        ),
        out_specs=(P("dp", "blk", None), P(("blk", "dp"), None)),
        check_vma=False,
    )
```

time: 472 us -> 312 us (0.66)
  waiting for transfers between devices: 362 us -> 0.01 us
  blocking collectives: 0 us -> 196 us
  Pallas kernels: 0 us -> 99.5 us
  matrix products: 28.9 us -> 0 us
  local copies, waits for them, and re-layouts: 25.3 us -> 5.36 us
  other arithmetic: 19.5 us -> 0.01 us
  between operations: 14.2 us -> 0.69 us
  starting transfers between devices: 19.4 us -> 8.53 us
    reduce_scatter x1 -> x0, waiting for transfers between devices: 197 us -> none  [per_device(): lax.psum_scatter(product * scale_factor, 'blk', scatter_dimension=0, tile...]
    all_gather x0 -> x1, blocking collectives: none -> 196 us  [per_device(): lax.all_gather(jnp.concatenate([shard_row, rows], axis=0), ('blk', 'dp'),...]
    all_gather x1 -> x0, waiting for transfers between devices: 114 us -> none  [per_device(): all_rows = lax.all_gather(own_rows, 'blk', axis=0, tiled=True)]
    pallas_call x0 -> x3, Pallas kernels: none -> 99.5 us  [the longest x1 90 us: per_device(): pl.pallas_call(main_kernel, out_shape=(jax.ShapeDtypeStruct((1, NQ, D), B...]
    all_to_all x2 -> x1, waiting for transfers between devices: 50.6 us -> 0.01 us  [per_device(): lax.all_to_all(slots, ('blk', 'dp'), split_axis=0, concat_axis=0, tiled=T...]
    dot_general x3 -> x0, matrix products: 28.9 us -> none  [the longest x1 10.8 us: per_device(): jnp.dot(coefficient, all_rows, preferred_element_type=jnp.float32)]
    scatter-add x1 -> x0, other arithmetic: 11.4 us -> none  [per_device(): jnp.zeros((HR, arrived.shape[1]), jnp.float32).at[landing]]
    gather x2 -> x0, local copies, waits for them, and re-layouts: 11.2 us -> none  [per_device(): buffer = jnp.take(padded_grad, inverse, axis=0)]
  transfers between devices with their start and end apart: 4 -> 1, of which waited for: 3 -> 0; matrix products, arithmetic and copies ran while one was open for 7% -> 0% of each run, Pallas kernels for 0% -> 1%
where the time goes in v1:
time: 312 us; the launch traced here: 310 us
  blocking collectives  196 us (63%)
  Pallas kernels  99.5 us (32%)
  starting transfers between devices  8.53 us (3%)
  local copies, waits for them, and re-layouts  5.36 us (2%)
    all_gather x1, blocking collectives, per_device(): lax.all_gather(jnp.concatenate([shard_row, rows], axis=0), ('blk', 'dp'),...  196 us
    pallas_call x1, Pallas kernels, per_device(): pl.pallas_call(main_kernel, out_shape=(jax.ShapeDtypeStruct((1, NQ, D), B...  90 us
    all_to_all x1, starting transfers between devices, per_device(): lax.all_to_all(slots, ('blk', 'dp'), split_axis=0, concat_axis=0, tiled=T...  8.53 us
    pallas_call x1, Pallas kernels, per_device(): pl.pallas_call(landing_kernel, out_shape=jax.ShapeDtypeStruct((HR, D), F3...  7.06 us
  transfers between devices with their start and end apart: 1, of which 0 were waited for; matrix products, arithmetic and copies ran while one was open for 0% of the time, Pallas kernels for 1%

profile of v1, /device:TPU:0, one launch (start us, length us, event | category | flops | bytes accessed | tf_op | source)
XLA Modules:
  0.0 310.5 jit_solution(5566733905254348074)
XLA Ops:
  0.6 1.4 copy.9.tcol_ref
  2.0 90.0 %gather_scores_reduce.1 = (bf16[1,1024,2560]{2,1,0:T(8,128)(2,1)}, bf16[128,16,640]{2,1,0:T(8,128)(2,1)}) custom-call(bf16[1,1024,2560]{2,1,0:T(8,128)(2,1)} %q_hbm.1, bf16[1,128,2560]{2,1,0:T(8,128)(2,1)} %c_hbm.1, f32[1,1024]{1,0:T(1,128)} %w_ref.1, s32[1,1024]{1,0:T(1,128)} %pos_ref.1, s32[1,128]{1,0:T(1,128)} %bitcast.14, s32[128,1]{1,0:T(8,128)} %copy.9.tcol_ref), custom_call_target="tpu_custom_call" | custom-call | flops 16106127360 | bytes 14680064 | tf_op jit(solution)/shard_map/gather_scores_reduce/pallas_call | solution.py:329
  92.0 0.0 copy-start.2
  92.0 0.0 copy-start.3
  92.0 8.5 %all-to-all-start = ((bf16[128,16,640]{2,1,0:T(8,128)(2,1)}), bf16[128,16,640]{2,1,0:T(8,128)(2,1)S(1)}, u32[]{:S(2)}, u32[]{:S(2)}) async-start(bf16[128,16,640]{2,1,0:T(8,128)(2,1)} %get-tuple-element.5), calls=%async_computation | async-start | bytes 5242880 | tf_op jit(solution)/shard_map/all_to_all | solution.py:367
  100.6 0.0 copy-done.2
  100.6 0.0 copy-done.3
  100.6 196.3 %all-gather.1 = s32[128,2,128]{2,1,0:T(2,128)S(1)} all-gather(s32[1,2,128]{2,1,0:T(2,128)S(1)} %add_bitcast_fusion), channel_id=2, replica_groups=mesh['blk'=8,'dp'=16] {'blk','dp'}, dimensions={0}, use_global_device_ids=true | all-gather | bytes 132096 | tf_op jit(solution)/shard_map/all_gather | solution.py:326
  296.9 0.8 fusion
  297.7 2.5 slot_rows.1.key_ref
  300.2 0.0 all-to-all-done.arrived_ref
  300.2 0.0 copy-start
  300.2 0.8 copy-done
  301.0 0.0 copy-start.1
  301.0 7.1 %landing.1 = f32[256,2560]{1,0:T(8,128)} custom-call(s32[8,2048]{1,0:T(8,128)S(1)} %copy-done, bf16[128,16,640]{2,1,0:T(8,128)(2,1)S(1)} %all-to-all-done.arrived_ref), custom_call_target="tpu_custom_call" | custom-call | tf_op jit(solution)/shard_map/landing/pallas_call | solution.py:376
  308.1 0.0 copy-done.1
  308.1 2.4 copy.15
  (1 shorter events, 0.0 us)
Async XLA Ops:
  92.0 8.6 %copy-start.2 = (s32[1,128,1]{1,2,0:T(1,128)S(1)}, s32[1,128,1]{1,2,0:T(1,128)}, u32[]{:S(2)}) copy-start(s32[1,128,1]{1,2,0:T(1,128)} %param.10) | copy-start | bytes 1540
  92.0 8.6 %copy-start.3 = (s32[1,128]{1,0:T(1,128)S(1)}, s32[1,128]{1,0:T(1,128)}, u32[]{:S(2)}) copy-start(s32[1,128]{1,0:T(1,128)} %param.11) | copy-start | bytes 1540
  92.0 208.2 %all-to-all-start = ((bf16[128,16,640]{2,1,0:T(8,128)(2,1)}), bf16[128,16,640]{2,1,0:T(8,128)(2,1)S(1)}, u32[]{:S(2)}, u32[]{:S(2)}) async-start(bf16[128,16,640]{2,1,0:T(8,128)(2,1)} %get-tuple-element.5), calls=%async_computation | async-start | bytes 5242880 | tf_op jit(solution)/shard_map/all_to_all | solution.py:367
  300.2 0.8 copy-start
  301.0 7.1 %copy-start.1 = (bf16[1,1024,2560]{2,1,0:T(8,128)(2,1)S(1)}, bf16[1,1024,2560]{2,1,0:T(8,128)(2,1)}, u32[]{:S(2)}) copy-start(bf16[1,1024,2560]{2,1,0:T(8,128)(2,1)} %get-tuple-element.10) | copy-start | bytes 15728644

commit v2 on v1

--- a/solution.py
+++ b/solution.py
@@ -32,11 +32,13 @@
 
 
 def main_kernel(
-    q_hbm, c_hbm, w_ref, pos_ref, trow_ref, tcol_ref, qg_hbm, slots_ref,
-    q, c, e, coef_t, coef, prod, snd, rcv, qg, sel, gs, mx, sm,
-    q_sem, c_sem, ag_send, ag_recv, rs_send, rs_recv, qg_sem,
+    q_hbm, c_hbm, w_ref, pos_ref, shard_ref, row_ref, qg_hbm, slots_ref, key_ref,
+    q, c, e, coef_t, coef, prod, snd, rcv, qg, sel, gs, mx, sm, told, heard,
+    q_sem, c_sem, ag_send, ag_recv, rs_send, rs_recv, qg_sem, tell_sem, hear_sem, self_sem,
 ):
-    blk = lax.axis_index("blk")
+    blk, dp = lax.axis_index("blk"), lax.axis_index("dp")
+    n_dp = lax.axis_size("dp")
+    me = blk * n_dp + dp
     z, x = blk // 2, blk % 2
 
     def at(dz, dx):
@@ -53,11 +55,19 @@
         copy.start()
 
     barrier = pltpu.get_barrier_semaphore()
-    for peer in peers.values():
+
+    def other(i):
+        peer = (me + i) % SHARDS
+        return peer, {"blk": peer // n_dp, "dp": peer % n_dp}
+
+    def greet(i, _):
         pl.semaphore_signal(
-            barrier, inc=1, device_id={"blk": peer}, device_id_type=pl.DeviceIdType.MESH
+            barrier, inc=1, device_id=other(i)[1], device_id_type=pl.DeviceIdType.MESH
         )
-    pl.semaphore_wait(barrier, 3)
+        return 0
+
+    lax.fori_loop(1, SHARDS, greet, 0)
+    pl.semaphore_wait(barrier, SHARDS - 1)
 
     def ag(src, dst, way):
         source = c_hbm.at[0, pl.ds(src * HB, HB)] if src < 2 else c.at[src]
@@ -81,12 +91,34 @@
     for slot in (ZM, ZP + 1, XN, ZM + 1, ZP, XN + 1):
         gather[slot].start()
 
-    earlier = (tcol_ref[...] == trow_ref[...]) & (
+    shard = shard_ref[...]
+    wide = jnp.broadcast_to(shard, (CB, CB))
+    earlier = (jnp.transpose(wide) == wide) & (
         lax.broadcasted_iota(I32, (CB, CB), 0) < lax.broadcasted_iota(I32, (CB, CB), 1)
     )
     place = jnp.sum(earlier.astype(I32), axis=0, keepdims=True)
-    slot_index = trow_ref[...] * MOST + place
+    slot_index = shard * MOST + place
     keys = jnp.concatenate([slot_index * 4 + part for part in range(4)], axis=1)
+
+    hit = (lax.broadcasted_iota(I32, (8 * SHARDS, CB), 0) // 8 == shard).astype(F32).astype(BF16)
+    number = jnp.where(
+        lax.broadcasted_iota(I32, (128, CB), 0) == place, row_ref[...] + 1, 0
+    ).astype(F32).astype(BF16)
+    told[...] = lax.dot_general(
+        hit, number, (((1,), (1,)), ((), ())), preferred_element_type=F32
+    ).astype(I32).reshape(SHARDS, 8, 128)
+
+    def tell(i, _):
+        peer, device = other(i)
+        pltpu.make_async_remote_copy(
+            src_ref=told.at[peer], dst_ref=heard.at[me], send_sem=tell_sem, recv_sem=hear_sem,
+            device_id=device, device_id_type=pl.DeviceIdType.MESH,
+        ).start()
+        return 0
+
+    lax.fori_loop(1, SHARDS, tell, 0)
+    note = pltpu.make_async_copy(told.at[me], heard.at[me], self_sem)
+    note.start()
 
     def fill(i, _):
         row = i * 256 + lax.broadcasted_iota(I32, (256, 4 * CB), 0)
@@ -237,6 +269,27 @@
             put(k, 11, prod[k, XN + 1] + got(k, 3) + got(k, 5))
             message(7, k).start()
 
+        @pl.when(i == 2)
+        def _():
+            pltpu.make_async_copy(
+                heard.at[pl.ds(0, SHARDS - 1)], heard.at[pl.ds(0, SHARDS - 1)], hear_sem
+            ).wait()
+            note.wait()
+            lanes = lax.broadcasted_iota(I32, (SHARDS, 16 * SHARDS), 1)
+            spread = lanes // 16 == lax.broadcasted_iota(I32, (SHARDS, 16 * SHARDS), 0)
+            unit = lax.broadcasted_iota(I32, (8, 128), 0) == lax.broadcasted_iota(I32, (8, 128), 1)
+            by_slot = lax.dot_general(
+                unit.astype(F32).astype(BF16), heard[:, 0, :].astype(F32).astype(BF16),
+                (((1,), (1,)), ((), ())), preferred_element_type=F32,
+            )
+            wide = jnp.dot(
+                by_slot.astype(BF16), spread.astype(F32).astype(BF16), preferred_element_type=F32
+            )
+            slot = lax.broadcasted_iota(I32, (8, 16 * SHARDS), 1) % 4
+            mine = lax.broadcasted_iota(I32, (8, 16 * SHARDS), 0) == slot
+            key = jnp.sum(jnp.where(mine, wide, 0.0), axis=0, keepdims=True).astype(I32) - 1
+            key_ref[...] = jnp.broadcast_to(key, (8, 16 * SHARDS))
+
         @pl.when((i >= 2) & (i <= NC + 1))
         def _():
             k = i - 2
@@ -278,28 +331,9 @@
         return 0
 
     lax.fori_loop(0, NC, drain, 0)
-
-
-def key_kernel(me_ref, shard_ref, row_ref, key_ref):
-    hits = (shard_ref[...] == me_ref[0]).astype(F32)
-    before = (
-        lax.broadcasted_iota(I32, (CB, CB), 0) < lax.broadcasted_iota(I32, (CB, CB), 1)
-    ).astype(F32)
-    place = jnp.dot(hits.astype(BF16), before.astype(BF16), preferred_element_type=F32)
-    numbers = (row_ref[...] + 1).astype(F32) * hits
-    lanes = lax.broadcasted_iota(I32, (SHARDS, 16 * SHARDS), 1)
-    spread = (lanes // 16 == lax.broadcasted_iota(I32, (SHARDS, 16 * SHARDS), 0)).astype(F32)
-    spread = spread.astype(BF16)
-    slot = lax.broadcasted_iota(I32, (8, 16 * SHARDS), 1) % 4
-    total = jnp.zeros((8, 16 * SHARDS), F32)
-    for k in range(MOST):
-        chosen = jnp.where(place == float(k), numbers, 0.0).astype(BF16)
-        by_source = lax.dot_general(
-            jnp.ones((8, CB), BF16), chosen, (((1,), (1,)), ((), ())), preferred_element_type=F32
-        )
-        wide = jnp.dot(by_source.astype(BF16), spread, preferred_element_type=F32)
-        total = total + jnp.where(slot == k, wide, 0.0)
-    key_ref[...] = total.astype(I32) - 1
+    pltpu.make_async_copy(
+        told.at[pl.ds(0, SHARDS - 1)], told.at[pl.ds(0, SHARDS - 1)], tell_sem
+    ).wait()
 
 
 def landing_kernel(key_ref, arrived_ref, out_ref, land):
@@ -322,18 +356,15 @@
 def per_device(queries, candidates, loss_weight, positives, producers, rows):
     vmem, hbm = pl.BlockSpec(memory_space=pltpu.VMEM), pl.BlockSpec(memory_space=pl.ANY)
     shard_row = producers.reshape(1, CB)
-    shard_column = producers.reshape(CB, 1)
-    meta = lax.all_gather(
-        jnp.concatenate([shard_row, rows], axis=0), ("blk", "dp"), axis=0, tiled=False
-    )
-    query_grad, slots = pl.pallas_call(
+    query_grad, slots, key = pl.pallas_call(
         main_kernel,
         out_shape=(
             jax.ShapeDtypeStruct((1, NQ, D), BF16),
             jax.ShapeDtypeStruct((SHARDS, 16, D // 4), BF16),
+            jax.ShapeDtypeStruct((8, 16 * SHARDS), I32),
         ),
         in_specs=[hbm, hbm, vmem, vmem, vmem, vmem],
-        out_specs=(hbm, vmem),
+        out_specs=(hbm, vmem, vmem),
         scratch_shapes=[
             pltpu.VMEM((NQ, D), BF16),
             pltpu.VMEM((16, HB, D), BF16),
@@ -348,6 +379,8 @@
             pltpu.VMEM((4 * CB, 128), BF16),
             pltpu.VMEM((8, NQ), F32),
             pltpu.VMEM((8, NQ), F32),
+            pltpu.VMEM((SHARDS, 8, 128), I32),
+            pltpu.VMEM((SHARDS, 8, 128), I32),
             pltpu.SemaphoreType.DMA,
             pltpu.SemaphoreType.DMA((2,)),
             pltpu.SemaphoreType.DMA((16,)),
@@ -355,6 +388,9 @@
             pltpu.SemaphoreType.DMA((NC, NM)),
             pltpu.SemaphoreType.DMA((NC, NM)),
             pltpu.SemaphoreType.DMA((NC,)),
+            pltpu.SemaphoreType.DMA,
+            pltpu.SemaphoreType.DMA,
+            pltpu.SemaphoreType.DMA,
         ],
         compiler_params=pltpu.CompilerParams(
             collective_id=0, has_side_effects=True, vmem_limit_bytes=60 * 2**20
@@ -363,16 +399,8 @@
             flops=6 * NQ * NQ * D, bytes_accessed=14 * 2**20, transcendentals=NQ * NQ
         ),
         name="gather_scores_reduce",
-    )(queries, candidates, loss_weight, positives, shard_row, shard_column)
+    )(queries, candidates, loss_weight, positives, shard_row, rows)
     arrived = lax.all_to_all(slots, ("blk", "dp"), split_axis=0, concat_axis=0, tiled=True)
-    me = lax.axis_index("blk") * lax.axis_size("dp") + lax.axis_index("dp")
-    key = pl.pallas_call(
-        key_kernel,
-        out_shape=jax.ShapeDtypeStruct((8, 16 * SHARDS), I32),
-        in_specs=[pl.BlockSpec(memory_space=pltpu.SMEM), vmem, vmem],
-        out_specs=vmem,
-        name="slot_rows",
-    )(me.astype(I32).reshape(1), meta[:, 0], meta[:, 1])
     decoder_grad = pl.pallas_call(
         landing_kernel,
         out_shape=jax.ShapeDtypeStruct((HR, D), F32),

time: 312 us -> 155 us (0.50)
  blocking collectives: 196 us -> 0 us
  waiting for transfers between devices: 0.01 us -> 35.7 us
  Pallas kernels: 99.5 us -> 110 us
    all_gather x1 -> x0, blocking collectives: 196 us -> none  [per_device(): lax.all_gather(jnp.concatenate([shard_row, rows], axis=0), ('blk', 'dp'),...]
    all_to_all x1, waiting for transfers between devices: 0.01 us -> 35.7 us  [per_device(): lax.all_to_all(slots, ('blk', 'dp'), split_axis=0, concat_axis=0, tiled=T...]
    pallas_call x1, Pallas kernels: 90 us -> 103 us  [per_device(): pl.pallas_call(main_kernel, out_shape=(jax.ShapeDtypeStruct((1, NQ, D), B...]
  transfers between devices with their start and end apart: 1 -> 1, of which waited for: 0 -> 1; matrix products, arithmetic and copies ran while one was open for 0% -> 0% of each run, Pallas kernels for 1% -> 0%
where the time goes in v2:
time: 155 us
  Pallas kernels  110 us (71%)
  waiting for transfers between devices  35.7 us (23%)
  starting transfers between devices  6.22 us (4%)
  local copies, waits for them, and re-layouts  2.37 us (2%)
    pallas_call x1, Pallas kernels, per_device(): pl.pallas_call(main_kernel, out_shape=(jax.ShapeDtypeStruct((1, NQ, D), B...  103 us
    all_to_all x1, waiting for transfers between devices, per_device(): lax.all_to_all(slots, ('blk', 'dp'), split_axis=0, concat_axis=0, tiled=T...  35.7 us
    pallas_call x1, Pallas kernels, per_device(): pl.pallas_call(landing_kernel, out_shape=jax.ShapeDtypeStruct((HR, D), F3...  7.06 us
    all_to_all x1, starting transfers between devices, per_device(): lax.all_to_all(slots, ('blk', 'dp'), split_axis=0, concat_axis=0, tiled=T...  6.22 us
  transfers between devices with their start and end apart: 1, of which 1 were waited for; matrix products, arithmetic and copies ran while one was open for 0% of the time, Pallas kernels for 0%

profile of v2, /device:TPU:0, one launch (start us, length us, event | category | flops | bytes accessed | tf_op | source)
XLA Modules:
  0.0 154.6 jit_solution(9734869622133422695)
XLA Ops:
  0.6 102.6 %gather_scores_reduce.1 = (bf16[1,1024,2560]{2,1,0:T(8,128)(2,1)}, bf16[128,16,640]{2,1,0:T(8,128)(2,1)}, s32[8,2048]{1,0:T(8,128)}) custom-call(bf16[1,1024,2560]{2,1,0:T(8,128)(2,1)} %q_hbm.1, bf16[1,128,2560]{2,1,0:T(8,128)(2,1)} %c_hbm.1, f32[1,1024]{1,0:T(1,128)} %w_ref.1, s32[1,1024]{1,0:T(1,128)} %pos_ref.1, s32[1,128]{1,0:T(1,128)} %bitcast.1, ...), custom_call_target="tpu_custom_call" | custom-call | flops 16106127360 | bytes 14680064 | tf_op jit(solution)/shard_map/gather_scores_reduce/pallas_call | solution.py:359
  103.2 0.0 copy-start
  103.3 6.2 %all-to-all-start = ((bf16[128,16,640]{2,1,0:T(8,128)(2,1)}), bf16[128,16,640]{2,1,0:T(8,128)(2,1)S(1)}, u32[]{:S(2)}, u32[]{:S(2)}) async-start(bf16[128,16,640]{2,1,0:T(8,128)(2,1)} %get-tuple-element.7), calls=%async_computation | async-start | bytes 5242880 | tf_op jit(solution)/shard_map/all_to_all | solution.py:403
  109.5 35.7 %all-to-all-done.arrived_ref = bf16[128,16,640]{2,1,0:T(8,128)(2,1)S(1)} async-done(((bf16[128,16,640]{2,1,0:T(8,128)(2,1)}), bf16[128,16,640]{2,1,0:T(8,128)(2,1)S(1)}, u32[]{:S(2)}, u32[]{:S(2)}) %all-to-all-start) | async-done | bytes 2621472 | tf_op jit(solution)/shard_map/all_to_all | solution.py:403
  145.2 0.0 copy-start.1
  145.2 0.0 copy-done
  145.2 7.1 %landing.1 = f32[256,2560]{1,0:T(8,128)} custom-call(s32[8,2048]{1,0:T(8,128)S(1)} %copy-done, bf16[128,16,640]{2,1,0:T(8,128)(2,1)S(1)} %all-to-all-done.arrived_ref), custom_call_target="tpu_custom_call" | custom-call | tf_op jit(solution)/shard_map/landing/pallas_call | solution.py:404
  152.3 0.0 copy-done.1
  152.3 2.4 %copy.9 = bf16[1,1024,2560]{2,1,0:T(8,128)(2,1)} copy(bf16[1,1024,2560]{2,1,0:T(8,128)(2,1)S(1)} %copy-done.1) | data formatting | bytes 10485760
Async XLA Ops:
  103.2 42.0 %copy-start = (s32[8,2048]{1,0:T(8,128)S(1)}, s32[8,2048]{1,0:T(8,128)}, u32[]{:S(2)}) copy-start(s32[8,2048]{1,0:T(8,128)} %get-tuple-element.6.key_ref) | copy-start | bytes 196612
  103.3 42.0 %all-to-all-start = ((bf16[128,16,640]{2,1,0:T(8,128)(2,1)}), bf16[128,16,640]{2,1,0:T(8,128)(2,1)S(1)}, u32[]{:S(2)}, u32[]{:S(2)}) async-start(bf16[128,16,640]{2,1,0:T(8,128)(2,1)} %get-tuple-element.7), calls=%async_computation | async-start | bytes 5242880 | tf_op jit(solution)/shard_map/all_to_all | solution.py:403
  145.2 7.1 %copy-start.1 = (bf16[1,1024,2560]{2,1,0:T(8,128)(2,1)S(1)}, bf16[1,1024,2560]{2,1,0:T(8,128)(2,1)}, u32[]{:S(2)}) copy-start(bf16[1,1024,2560]{2,1,0:T(8,128)(2,1)} %get-tuple-element.10) | copy-start | bytes 15728644

commit v3 on v1

v3 whole, which is shorter than its diff:
```python
import functools
import math

import jax
import jax.numpy as jnp
from jax import lax
from jax.experimental import pallas as pl
from jax.experimental.pallas import tpu as pltpu
from jax.sharding import PartitionSpec as P

D = 2560
HR = 256
MOST = 4
NQ = 1024
CB = 128
HB = 64
NC = 5
CW = D // NC
SHARDS = 128
SCALE = 1.0 / math.sqrt(D)
F32, BF16, I32 = jnp.float32, jnp.bfloat16, jnp.int32

SELF, XN, ZP, ZM, Z2 = 0, 2, 4, 6, 8
ZPX, ZMX, Z2X = (10, 13), (11, 14), (12, 15)
GROUPS = ((0, 4), (4, 4), (8, 5), (13, 3))

MESSAGES = (
    (0, 2, "x"), (2, 2, "p"), (4, 2, "m"), (6, 1, "p"), (7, 1, "m"),
    (8, 1, "p"), (9, 1, "m"), (10, 2, "x"), (12, 1, "p"), (13, 1, "m"),
)
NM = len(MESSAGES)
KEEP = {SELF: 0, SELF + 1: 1, XN: 2, XN + 1: 3, ZP: 4, ZP + 1: 5, ZM: 6, ZM + 1: 7, Z2: 8, Z2 + 1: 9}
FAR = (2, 1, 3, 0)


def main_kernel(
    q_hbm, c_hbm, w_ref, pos_ref, shard_ref, row_ref, qg_hbm, out_hbm,
    q, c, e, coef_t, coef, prod, snd, rcv, qg, sel, gs, mx, sm, meta, land, out,
    near, cross, from_core, from_x, from_y, from_z,
    q_sem, c_sem, ag_send, ag_recv, rs_send, rs_recv, qg_sem, out_sem,
    meta_send, meta_recv, slot_send, core_recv, x_recv, y_recv, z_recv,
):
    blk, dp = lax.axis_index("blk"), lax.axis_index("dp")
    z, x_lo = lax.div(blk, 2), lax.rem(blk, 2)
    x_hi, y, core = lax.div(dp, 8), lax.rem(lax.div(dp, 2), 4), lax.rem(dp, 2)
    x = x_hi * 2 + x_lo

    def at(dz, dx):
        return lax.rem(z + dz, 4) * 2 + lax.rem(x_lo + dx, 2)

    def device(dz=0, dy=0, dx=0, dc=0):
        across = lax.rem(x + dx, 4)
        return {
            "blk": lax.rem(z + dz, 4) * 2 + lax.rem(across, 2),
            "dp": lax.div(across, 2) * 8 + lax.rem(y + dy, 4) * 2 + lax.rem(core + dc, 2),
        }

    def to(src, dst, send, recv, **way):
        return pltpu.make_async_remote_copy(
            src_ref=src, dst_ref=dst, send_sem=send, recv_sem=recv,
            device_id=device(**way), device_id_type=pl.DeviceIdType.MESH,
        )

    def whole(ref, sem):
        pltpu.make_async_copy(ref, ref, sem).wait()

    peers = {"x": at(0, 1), "p": at(1, 0), "m": at(3, 0)}

    q_copy = pltpu.make_async_copy(q_hbm.at[0], q, q_sem)
    q_copy.start()
    own = [
        pltpu.make_async_copy(c_hbm.at[0, pl.ds(h * HB, HB)], c.at[h], c_sem.at[h]) for h in (0, 1)
    ]
    for copy in own:
        copy.start()

    meta[0, 0, 0, 0, 0:1, :] = shard_ref[...]
    meta[0, 0, 0, 0, 1:2, :] = row_ref[...]
    lines = [{"dc": 1}] + [{axis: far} for axis in ("dx", "dy", "dz") for far in (1, 2, 3)]
    barrier = pltpu.get_barrier_semaphore()
    for line in lines:
        pl.semaphore_signal(
            barrier, inc=1, device_id=device(**line), device_id_type=pl.DeviceIdType.MESH
        )
    pl.semaphore_wait(barrier, len(lines))

    def ag(src, dst, way):
        source = c_hbm.at[0, pl.ds(src * HB, HB)] if src < 2 else c.at[src]
        return pltpu.make_async_remote_copy(
            src_ref=source,
            dst_ref=c.at[dst],
            send_sem=ag_send.at[dst],
            recv_sem=ag_recv.at[dst],
            device_id={"blk": peers[way]},
            device_id_type=pl.DeviceIdType.MESH,
        )

    gather = {
        ZM: ag(0, ZM, "p"), ZP + 1: ag(1, ZP + 1, "m"), XN: ag(0, XN, "x"),
        ZM + 1: ag(1, ZM + 1, "p"), ZP: ag(0, ZP, "m"), XN + 1: ag(1, XN + 1, "x"),
        Z2: ag(ZM, Z2, "p"), Z2 + 1: ag(ZP + 1, Z2 + 1, "m"),
        ZMX[0]: ag(XN, ZMX[0], "p"), ZPX[0]: ag(XN, ZPX[0], "m"),
        ZMX[1]: ag(XN + 1, ZMX[1], "p"), ZPX[1]: ag(XN + 1, ZPX[1], "m"),
        Z2X[0]: ag(Z2, Z2X[0], "x"), Z2X[1]: ag(Z2 + 1, Z2X[1], "x"),
    }
    for slot in (ZM, ZP + 1, XN, ZM + 1, ZP, XN + 1):
        gather[slot].start()

    def tell(k, src, dst, **way):
        return to(src, dst, meta_send.at[k], meta_recv.at[k], **way)

    tell_core = [tell(0, meta.at[0, 0, 0, 0], meta.at[0, 0, 0, 1], dc=1)]
    tell_x = [tell(far, meta.at[0, 0, 0], meta.at[0, 0, far], dx=far) for far in (1, 2, 3)]
    tell_y = [tell(3 + far, meta.at[0, 0], meta.at[0, far], dy=far) for far in (1, 2, 3)]
    tell_z = [tell(6 + far, meta.at[0], meta.at[far], dz=far) for far in (1, 2, 3)]
    for copy in tell_core:
        copy.start()

    shard = shard_ref[...]
    wide = jnp.broadcast_to(shard, (CB, CB))
    earlier = (jnp.transpose(wide) == wide) & (
        lax.broadcasted_iota(I32, (CB, CB), 0) < lax.broadcasted_iota(I32, (CB, CB), 1)
    )
    place = jnp.sum(earlier.astype(I32), axis=0, keepdims=True)
    slot_index = shard * MOST + place
    keys = jnp.concatenate([slot_index * 4 + part for part in range(4)], axis=1)

    def fill(i, _):
        row = i * 256 + lax.broadcasted_iota(I32, (256, 1), 0)
        number = row // 16
        inside = number % 64
        rest = jnp.maximum(inside - 16, 0)
        straight = inside < 16
        dc = (number < 64).astype(I32)
        dz = jnp.where(straight, inside // 4, rest // 12)
        dx = jnp.where(straight, 0, 1 + (rest % 12) // 4)
        across = (x + dx) % 4
        to_shard = ((z + dz) % 4 * 2 + across % 2) * 16 + (
            across // 2 * 8 + (y + inside % 4) % 4 * 2 + (core + dc) % 2
        )
        key = (to_shard * MOST + row % 4) * 4 + (row // 4) % 4
        sel[pl.ds(pl.multiple_of(i * 256, 256), 256), :] = (key == keys).astype(F32).astype(BF16)
        return 0

    lax.fori_loop(0, 16 * SHARDS // 256, fill, 0)
    for copy in tell_core:
        copy.wait_recv()
    for copy in tell_x:
        copy.start()
    q_copy.wait()
    for copy in own:
        copy.wait()

    def scores(which):
        first, number = GROUPS[which]

        def part(i, _):
            span = pl.ds(pl.multiple_of(i * 256, 256), 256)
            s = lax.dot_general(
                c[first : first + number].reshape(number * HB, D), q[span, :],
                (((1,), (1,)), ((), ())), preferred_element_type=F32,
            ) * SCALE
            top = jnp.max(s, axis=0, keepdims=True)
            shifted = jnp.exp(s - top)
            e[first : first + number, :, span] = shifted.reshape(number, HB, 256)
            mx[which : which + 1, span] = top
            sm[which : which + 1, span] = jnp.sum(shifted, axis=0, keepdims=True)
            return 0

        lax.fori_loop(0, NQ // 256, part, 0)

    gather[ZM].wait_recv()
    gather[Z2].start()
    gather[ZP + 1].wait_recv()
    gather[Z2 + 1].start()
    gather[XN].wait_recv()
    gather[XN + 1].wait_recv()
    scores(0)
    for copy in tell_x:
        copy.wait_recv()
    for copy in tell_y:
        copy.start()
    gather[ZM + 1].wait_recv()
    gather[ZP].wait_recv()
    scores(1)
    for copy in tell_y:
        copy.wait_recv()
    for copy in tell_z:
        copy.start()
    gather[Z2].wait_recv()
    gather[Z2X[0]].start()
    gather[Z2 + 1].wait_recv()
    gather[Z2X[1]].start()
    for slot in (ZMX[0], ZPX[0], ZMX[1], ZPX[1]):
        gather[slot].start()
    for slot in (ZPX[0], ZMX[0], Z2X[0]):
        gather[slot].wait_recv()
    scores(2)
    for slot in (ZPX[1], ZMX[1], Z2X[1]):
        gather[slot].wait_recv()
    scores(3)

    top = jnp.max(mx[0:4], axis=0, keepdims=True)
    rescale = jnp.exp(mx[0:4] - top)
    inverse = 1.0 / jnp.sum(rescale * sm[0:4], axis=0, keepdims=True)
    weight, target = w_ref[...], pos_ref[...]
    places = {
        0: at(0, 0), 2: at(0, 1), 4: at(1, 0), 6: at(3, 0), 8: at(2, 0),
    }
    starts = [0] * 16
    for first, owner in places.items():
        starts[first], starts[first + 1] = owner * CB, owner * CB + HB
    for (low, high), owner in ((ZPX, at(1, 1)), (ZMX, at(3, 1)), (Z2X, at(2, 1))):
        starts[low], starts[high] = owner * CB, owner * CB + HB
    for which, (first, number) in enumerate(GROUPS):
        factor = rescale[which : which + 1] * inverse
        for k in range(first, first + number):
            ids = starts[k] + lax.broadcasted_iota(I32, (HB, NQ), 0)
            onehot = (ids == target).astype(F32)
            coef_t[k] = (weight * (e[k] * factor - onehot)).astype(BF16)

    def message(m, chunk):
        first, number, way = MESSAGES[m]
        return pltpu.make_async_remote_copy(
            src_ref=snd.at[chunk, pl.ds(first, number)],
            dst_ref=rcv.at[chunk, pl.ds(first, number)],
            send_sem=rs_send.at[chunk, m],
            recv_sem=rs_recv.at[chunk, m],
            device_id={"blk": peers[way]},
            device_id_type=pl.DeviceIdType.MESH,
        )

    def qg_copy(chunk):
        return pltpu.make_async_copy(
            qg.at[lax.rem(chunk, 2)],
            qg_hbm.at[0, :, pl.ds(pl.multiple_of(chunk * CW, CW), CW)],
            qg_sem.at[lax.rem(chunk, 2)],
        )

    def put(chunk, slot, value):
        snd[chunk, slot] = value.astype(BF16)

    def got(chunk, slot):
        return rcv[chunk, slot].astype(F32)

    def kept(chunk, slot):
        return prod[lax.rem(chunk, 4), KEEP[slot]]

    def core_copies(k):
        send, recv = slot_send.at[k, 0], core_recv
        return [
            to(near.at[k], from_x.at[k, :, 0, 1], send, recv.at[k, 0], dc=1),
            to(cross.at[k], from_core.at[k, :, :, 1], send, recv.at[k, 1], dc=1),
        ]

    def x_leg(k):
        for copy in core_copies(k):
            copy.wait_recv()
        for dz in FAR:
            for far in (1, 2, 3):
                to(from_core.at[k, dz, far - 1], from_x.at[k, dz, far],
                   slot_send.at[k, 1], x_recv.at[k, dz], dx=far).start()

    def y_leg(k, dz):
        whole(from_x.at[k, dz, pl.ds(1, 3)], x_recv.at[k, dz])
        for far in (1, 2, 3):
            to(from_x.at[k, dz, :, :, far], from_y.at[k, dz, far - 1],
               slot_send.at[k, 2], y_recv.at[k, dz], dy=far).start()

    def z_leg(k, dz):
        whole(from_y.at[k, dz], y_recv.at[k, dz])
        if dz:
            to(from_x.at[k, dz, :, :, 0], from_z.at[k, dz - 1, 0],
               slot_send.at[k, 3], z_recv.at[k, dz - 1], dz=dz).start()
            to(from_y.at[k, dz], from_z.at[k, dz - 1, pl.ds(1, 3)],
               slot_send.at[k, 3], z_recv.at[k, dz - 1], dz=dz).start()

    def out_copy(chunk):
        return pltpu.make_async_copy(
            out.at[chunk],
            out_hbm.at[:, pl.ds(pl.multiple_of(chunk * CW, CW), CW)],
            out_sem.at[chunk],
        )

    def touch_down(chunk):
        for dz in (1, 2, 3):
            whole(from_z.at[chunk, dz - 1], z_recv.at[chunk, dz - 1])
        total = jnp.dot(
            land[:, 0:1536], from_z[chunk].reshape(1536, 128), preferred_element_type=F32
        )
        total += jnp.dot(
            land[:, 1536:1920], from_y[chunk, 0].reshape(384, 128), preferred_element_type=F32
        )
        total += jnp.dot(
            land[:, 1920:2048], from_x[chunk, 0, :, :, 0].reshape(128, 128),
            preferred_element_type=F32,
        )
        for part in range(4):
            out[chunk, :, part * 128 : part * 128 + 128] = total[part * HR : part * HR + HR]
        out_copy(chunk).start()

    def landing_rows():
        for copy in tell_z:
            copy.wait_recv()
        everyone = meta[...].reshape(SHARDS, 2, CB)
        order = [everyone[32:128], everyone[8:32], everyone[0:8]]
        shards = jnp.concatenate([part[:, 0, :] for part in order], axis=0)
        numbers = jnp.concatenate([part[:, 1, :] for part in order], axis=0)
        hits = (shards == blk * 16 + dp).astype(F32)
        before = (
            lax.broadcasted_iota(I32, (CB, CB), 0) < lax.broadcasted_iota(I32, (CB, CB), 1)
        ).astype(F32).astype(BF16)
        spot = jnp.dot(hits.astype(BF16), before, preferred_element_type=F32)
        numbers = (numbers + 1).astype(F32) * hits
        lanes = lax.broadcasted_iota(I32, (SHARDS, 16 * SHARDS), 1)
        spread = lanes // 16 == lax.broadcasted_iota(I32, (SHARDS, 16 * SHARDS), 0)
        spread = spread.astype(F32).astype(BF16)
        slot = lax.broadcasted_iota(I32, (8, 16 * SHARDS), 1) % 4
        key = jnp.zeros((8, 16 * SHARDS), F32)
        for k in range(MOST):
            chosen = jnp.where(spot == float(k), numbers, 0.0).astype(BF16)
            by_source = lax.dot_general(
                jnp.ones((8, CB), BF16), chosen, (((1,), (1,)), ((), ())),
                preferred_element_type=F32,
            )
            by_slot = jnp.dot(by_source.astype(BF16), spread, preferred_element_type=F32)
            key = key + jnp.where(slot == k, by_slot, 0.0)
        key = key[0:1].astype(I32) - 1
        part = (lax.broadcasted_iota(I32, (1, 16 * SHARDS), 1) // 4) % 4
        for k in range(4):
            mine = jnp.where(part == k, key, -1)
            for half in range(HR // 64):
                rows = half * 64 + lax.broadcasted_iota(I32, (64, 16 * SHARDS), 0)
                first = k * HR + half * 64
                land[first : first + 64, :] = (rows == mine).astype(F32).astype(BF16)

    def step(i, _):
        @pl.when(i < NC)
        def _():
            slab = lax.rem(i, 4)
            for half in range(CW // 256):
                columns = pl.ds(pl.multiple_of(i * CW + half * 256, 256), 256)
                span = slice(half * 256, half * 256 + 256)
                block = jnp.dot(
                    coef_t[...].reshape(16 * HB, NQ), q[:, columns], preferred_element_type=F32
                ) * SCALE
                block = block.reshape(16, HB, 256)
                for slot, k in KEEP.items():
                    prod[slab, k, :, span] = block[slot]
                for k, slot in enumerate(Z2X + ZPX + ZMX):
                    snd[i, k, :, span] = block[slot].astype(BF16)
                snd[i, 6, :, span] = block[ZP].astype(BF16)
                snd[i, 7, :, span] = block[ZM + 1].astype(BF16)
            for m in range(5):
                message(m, i).start()

        @pl.when((i >= 1) & (i <= NC))
        def _():
            k = i - 1
            message(0, k).wait_recv()
            put(k, 9, kept(k, Z2) + got(k, 0))
            message(6, k).start()
            put(k, 8, kept(k, Z2 + 1) + got(k, 1))
            message(5, k).start()
            message(1, k).wait_recv()
            message(2, k).wait_recv()
            put(k, 10, kept(k, XN) + got(k, 2) + got(k, 4))
            put(k, 11, kept(k, XN + 1) + got(k, 3) + got(k, 5))
            message(7, k).start()

        @pl.when((i >= 2) & (i <= NC + 1))
        def _():
            k = i - 2
            message(5, k).wait_recv()
            put(k, 12, kept(k, ZP + 1) + got(k, 8))
            message(8, k).start()
            message(6, k).wait_recv()
            put(k, 13, kept(k, ZM) + got(k, 9))
            message(9, k).start()

        @pl.when((i >= 3) & (i <= NC + 2))
        def _():
            k = i - 3
            for m in (3, 4, 7, 8, 9):
                message(m, k).wait_recv()
            low = kept(k, SELF) + got(k, 6) + got(k, 13) + got(k, 10)
            high = kept(k, SELF + 1) + got(k, 7) + got(k, 12) + got(k, 11)
            for part in range(4):
                lanes = slice(part * 128, part * 128 + 128)
                gs[part * CB : part * CB + HB, :] = low[:, lanes].astype(BF16)
                gs[part * CB + HB : part * CB + CB, :] = high[:, lanes].astype(BF16)
            picked = jnp.dot(sel[...], gs[...], preferred_element_type=F32).astype(BF16)
            near[k] = picked[0:256].reshape(4, 4, 16, 128)
            cross[k] = picked[256:1024].reshape(4, 3, 4, 16, 128)
            from_x[k, :, 0, 0] = picked[1024:1280].reshape(4, 4, 16, 128)
            from_core[k, :, :, 0] = picked[1280:2048].reshape(4, 3, 4, 16, 128)
            for copy in core_copies(k):
                copy.start()

        @pl.when((i >= 4) & (i <= NC + 3))
        def _():
            x_leg(i - 4)

        @pl.when((i >= 5) & (i <= NC + 4))
        def _():
            for dz in FAR:
                y_leg(i - 5, dz)

        @pl.when((i >= 6) & (i <= NC + 4))
        def _():
            for dz in FAR:
                z_leg(i - 6, dz)

        @pl.when(i == 0)
        def _():
            for k in range(4):
                coef[pl.ds(k * 256, 256), :] = jnp.transpose(
                    coef_t[:, :, k * 256 : k * 256 + 256].reshape(16 * HB, 256)
                )

        @pl.when(i < NC)
        def _():
            @pl.when(i >= 2)
            def _():
                qg_copy(i - 2).wait()

            for half in range(CW // 256):
                columns = pl.ds(pl.multiple_of(i * CW + half * 256, 256), 256)
                total = jnp.dot(
                    coef[...], c[:, :, columns].reshape(16 * HB, 256), preferred_element_type=F32
                )
                qg[lax.rem(i, 2), :, half * 256 : half * 256 + 256] = (total * SCALE).astype(BF16)
            qg_copy(i).start()

        @pl.when(i == 2)
        def _():
            landing_rows()

        @pl.when((i >= 7) & (i <= NC + 4))
        def _():
            touch_down(i - 7)

        return 0

    lax.fori_loop(0, NC + 5, step, 0)
    for dz in FAR:
        z_leg(NC - 1, dz)
    for chunk in (NC - 2, NC - 1):
        touch_down(chunk)

    for copy in gather.values():
        copy.wait_send()

    for copy in tell_core + tell_x + tell_y + tell_z:
        copy.wait_send()

    def drain(i, _):
        for m in range(NM):
            message(m, i).wait_send()
        whole(from_x.at[i, pl.ds(0, 2)], slot_send.at[i, 0])
        whole(from_core.at[i], slot_send.at[i, 1])
        whole(from_y.at[i], slot_send.at[i, 2])
        whole(from_z.at[i], slot_send.at[i, 3])
        out_copy(i).wait()
        return 0

    lax.fori_loop(0, NC, drain, 0)
    qg_copy(NC - 2).wait()
    qg_copy(NC - 1).wait()


def per_device(queries, candidates, loss_weight, positives, producers, rows):
    vmem, hbm = pl.BlockSpec(memory_space=pltpu.VMEM), pl.BlockSpec(memory_space=pl.ANY)
    shard_row = producers.reshape(1, CB)
    return pl.pallas_call(
        main_kernel,
        out_shape=(
            jax.ShapeDtypeStruct((1, NQ, D), BF16),
            jax.ShapeDtypeStruct((HR, D), F32),
        ),
        in_specs=[hbm, hbm, vmem, vmem, vmem, vmem],
        out_specs=(hbm, hbm),
        scratch_shapes=[
            pltpu.VMEM((NQ, D), BF16),
            pltpu.VMEM((16, HB, D), BF16),
            pltpu.VMEM((16, HB, NQ), F32),
            pltpu.VMEM((16, HB, NQ), BF16),
            pltpu.VMEM((NQ, 16 * HB), BF16),
            pltpu.VMEM((4, len(KEEP), HB, CW), F32),
            pltpu.VMEM((NC, 14, HB, CW), BF16),
            pltpu.VMEM((NC, 14, HB, CW), BF16),
            pltpu.VMEM((2, NQ, CW), BF16),
            pltpu.VMEM((16 * SHARDS, 4 * CB), BF16),
            pltpu.VMEM((4 * CB, 128), BF16),
            pltpu.VMEM((8, NQ), F32),
            pltpu.VMEM((8, NQ), F32),
            pltpu.VMEM((4, 4, 4, 2, 2, CB), I32),
            pltpu.VMEM((4 * HR, 16 * SHARDS), BF16),
            pltpu.VMEM((NC, HR, CW), F32),
            pltpu.VMEM((NC, 4, 4, 16, 128), BF16),
            pltpu.VMEM((NC, 4, 3, 4, 16, 128), BF16),
            pltpu.VMEM((NC, 4, 3, 2, 4, 16, 128), BF16),
            pltpu.VMEM((NC, 4, 4, 2, 4, 16, 128), BF16),
            pltpu.VMEM((NC, 4, 3, 4, 2, 16, 128), BF16),
            pltpu.VMEM((NC, 3, 4, 4, 2, 16, 128), BF16),
            pltpu.SemaphoreType.DMA,
            pltpu.SemaphoreType.DMA((2,)),
            pltpu.SemaphoreType.DMA((16,)),
            pltpu.SemaphoreType.DMA((16,)),
            pltpu.SemaphoreType.DMA((NC, NM)),
            pltpu.SemaphoreType.DMA((NC, NM)),
            pltpu.SemaphoreType.DMA((2,)),
            pltpu.SemaphoreType.DMA((NC,)),
            pltpu.SemaphoreType.DMA((10,)),
            pltpu.SemaphoreType.DMA((10,)),
            pltpu.SemaphoreType.DMA((NC, 4)),
            pltpu.SemaphoreType.DMA((NC, 2)),
            pltpu.SemaphoreType.DMA((NC, 4)),
            pltpu.SemaphoreType.DMA((NC, 4)),
            pltpu.SemaphoreType.DMA((NC, 3)),
        ],
        compiler_params=pltpu.CompilerParams(
            collective_id=0, has_side_effects=True, vmem_limit_bytes=62 * 2**20
        ),
        cost_estimate=pl.CostEstimate(
            flops=6 * NQ * NQ * D, bytes_accessed=20 * 2**20, transcendentals=NQ * NQ
        ),
        name="listwise_backward",
    )(queries, candidates, loss_weight, positives, shard_row, rows)


def solution(mesh):
    return jax.shard_map(
        per_device,
        mesh=mesh,
        in_specs=(
            P("dp", "blk", None),
            P("dp", "blk", None),
            P("dp", "blk"),
            P("dp", "blk"),
            P("dp", "blk", None),
            P("dp", "blk"),
        ),
        out_specs=(P("dp", "blk", None), P(("blk", "dp"), None)),
        check_vma=False,
    )
```

time: 312 us -> 137 us (0.44)
  blocking collectives: 196 us -> 0 us
  Pallas kernels: 99.5 us -> 130 us
  starting transfers between devices: 8.53 us -> 0 us
    all_gather x1 -> x0, blocking collectives: 196 us -> none  [per_device(): lax.all_gather(jnp.concatenate([shard_row, rows], axis=0), ('blk', 'dp'),...]
    pallas_call x1, Pallas kernels: 90 us -> 130 us  [per_device(): pl.pallas_call(main_kernel, out_shape=(jax.ShapeDtypeStruct((1, NQ, D), B...]
    pallas_call x2 -> x0, Pallas kernels: 9.55 us -> none  [the longest x1 7.06 us: per_device(): pl.pallas_call(landing_kernel, out_shape=jax.ShapeDtypeStruct((HR, D), F3...]
    all_to_all x1 -> x0, starting transfers between devices: 8.53 us -> none  [per_device(): lax.all_to_all(slots, ('blk', 'dp'), split_axis=0, concat_axis=0, tiled=T...]
    unnamed x9 -> x4, local copies, waits for them, and re-layouts: 3.21 us -> 6.83 us
  transfers between devices with their start and end apart: 1 -> 0, of which waited for: 0 -> 0; matrix products, arithmetic and copies ran while one was open for 0% -> 0% of each run, Pallas kernels for 1% -> 0%
where the time goes in v3:
time: 137 us
  Pallas kernels  130 us (95%)
  local copies, waits for them, and re-layouts  6.83 us (5%)
    pallas_call x1, Pallas kernels, per_device(): pl.pallas_call(main_kernel, out_shape=(jax.ShapeDtypeStruct((1, NQ, D), B...  130 us
    unnamed x4, local copies, waits for them, and re-layouts  6.83 us

profile of v3, /device:TPU:0, one launch (start us, length us, event | category | flops | bytes accessed | tf_op | source)
XLA Modules:
  0.0 137.3 jit_solution(5167991076265585589)
XLA Ops:
  0.6 129.8 %listwise_backward.1 = (bf16[1,1024,2560]{2,1,0:T(8,128)(2,1)}, f32[256,2560]{1,0:T(8,128)}) custom-call(bf16[1,1024,2560]{2,1,0:T(8,128)(2,1)} %q_hbm.1, bf16[1,128,2560]{2,1,0:T(8,128)(2,1)} %c_hbm.1, f32[1,1024]{1,0:T(1,128)} %w_ref.1, s32[1,1024]{1,0:T(1,128)} %pos_ref.1, s32[1,128]{1,0:T(1,128)} %bitcast.1, s32[1,128]{1,0:T(1,128)} %row_ref.1), custom_call_target="tpu_custom_call" | custom-call | flops 16106127360 | bytes 20971520 | tf_op jit(solution)/shard_map/listwise_backward/pallas_call | solution.py:475
  130.4 0.0 copy-start
  130.4 5.3 %copy.10 = bf16[1,1024,2560]{2,1,0:T(8,128)(2,1)} copy(bf16[1,1024,2560]{2,1,0:T(8,128)(2,1)} %get-tuple-element.4) | data formatting | bytes 10485760
  135.8 0.0 copy-done
  135.8 1.5 %copy.11 = f32[256,2560]{1,0:T(8,128)} copy(f32[256,2560]{1,0:T(8,128)S(1)} %copy-done) | data formatting | bytes 5242880
Async XLA Ops:
  130.4 5.3 %copy-start = (f32[256,2560]{1,0:T(8,128)S(1)}, f32[256,2560]{1,0:T(8,128)}, u32[]{:S(2)}) copy-start(f32[256,2560]{1,0:T(8,128)} %get-tuple-element.5) | copy-start | bytes 7864324

commit v4 on v3

v4 whole, which is shorter than its diff:
```python
import functools
import math

import jax
import jax.numpy as jnp
from jax import lax
from jax.experimental import pallas as pl
from jax.experimental.pallas import tpu as pltpu
from jax.sharding import PartitionSpec as P

D = 2560
HR = 256
MOST = 4
NQ = 1024
CB = 128
HB = 64
NC = 5
CW = D // NC
ND = 5
PER = NC // ND
QW = 512
BW = D // ND // 2
SHARDS = 128
SCALE = 1.0 / math.sqrt(D)
F32, BF16, I32 = jnp.float32, jnp.bfloat16, jnp.int32

SELF, XN, ZP, ZM, Z2 = 0, 2, 4, 6, 8
ZPX, ZMX, Z2X = (10, 13), (11, 14), (12, 15)
GROUPS = ((0, 4), (4, 4), (8, 5), (13, 3))

MESSAGES = (
    (0, 2, "x"), (2, 2, "p"), (4, 2, "m"), (6, 1, "p"), (7, 1, "m"),
    (8, 1, "p"), (9, 1, "m"), (10, 2, "x"), (12, 1, "p"), (13, 1, "m"),
)
NM = len(MESSAGES)
KEEP = {SELF: 0, SELF + 1: 1, XN: 2, XN + 1: 3, ZP: 4, ZP + 1: 5, ZM: 6, ZM + 1: 7, Z2: 8, Z2 + 1: 9}
PAIRS = SHARDS // 2

AWAY = sorted(
    ((n // 16, n // 4 % 4, n % 4) for n in range(1, PAIRS)),
    key=lambda way: -sum(min(far, 4 - far) for far in way),
)


def main_kernel(
    q_hbm, c_hbm, w_ref, pos_ref, shard_ref, row_ref, qg_hbm, out_hbm,
    q, c, e, coef_t, coef, prod, snd, rcv, qg, sel, mx, sm, meta, land, out,
    grad, sent, landed,
    q_sem, c_sem, ag_send, ag_recv, rs_send, rs_recv, qg_sem, out_sem,
    meta_send, meta_recv, core_send, core_recv, slot_send, slot_recv,
):
    blk, dp = lax.axis_index("blk"), lax.axis_index("dp")
    z, x_lo = lax.div(blk, 2), lax.rem(blk, 2)
    x_hi, y, core = lax.div(dp, 8), lax.rem(lax.div(dp, 2), 4), lax.rem(dp, 2)
    x = x_hi * 2 + x_lo

    def at(dz, dx):
        return lax.rem(z + dz, 4) * 2 + lax.rem(x_lo + dx, 2)

    def device(dz=0, dy=0, dx=0, dc=0):
        across = lax.rem(x + dx, 4)
        return {
            "blk": lax.rem(z + dz, 4) * 2 + lax.rem(across, 2),
            "dp": lax.div(across, 2) * 8 + lax.rem(y + dy, 4) * 2 + lax.rem(core + dc, 2),
        }

    def to(src, dst, send, recv, **way):
        return pltpu.make_async_remote_copy(
            src_ref=src, dst_ref=dst, send_sem=send, recv_sem=recv,
            device_id=device(**way), device_id_type=pl.DeviceIdType.MESH,
        )

    def whole(ref, sem):
        pltpu.make_async_copy(ref, ref, sem).wait()

    peers = {"x": at(0, 1), "p": at(1, 0), "m": at(3, 0)}

    q_copy = pltpu.make_async_copy(q_hbm.at[0], q, q_sem)
    q_copy.start()
    own = [
        pltpu.make_async_copy(c_hbm.at[0, pl.ds(h * HB, HB)], c.at[h], c_sem.at[h]) for h in (0, 1)
    ]
    for copy in own:
        copy.start()

    meta[0, 0, 0, 0, 0:1, :] = shard_ref[...]
    meta[0, 0, 0, 0, 1:2, :] = row_ref[...]
    lines = [{"dc": 1}] + [{"dz": dz, "dy": dy, "dx": dx} for dz, dy, dx in AWAY]
    barrier = pltpu.get_barrier_semaphore()
    for line in lines:
        pl.semaphore_signal(
            barrier, inc=1, device_id=device(**line), device_id_type=pl.DeviceIdType.MESH
        )
    pl.semaphore_wait(barrier, len(lines))

    def ag(src, dst, way):
        source = c_hbm.at[0, pl.ds(src * HB, HB)] if src < 2 else c.at[src]
        return pltpu.make_async_remote_copy(
            src_ref=source,
            dst_ref=c.at[dst],
            send_sem=ag_send.at[dst],
            recv_sem=ag_recv.at[dst],
            device_id={"blk": peers[way]},
            device_id_type=pl.DeviceIdType.MESH,
        )

    gather = {
        ZM: ag(0, ZM, "p"), ZP + 1: ag(1, ZP + 1, "m"), XN: ag(0, XN, "x"),
        ZM + 1: ag(1, ZM + 1, "p"), ZP: ag(0, ZP, "m"), XN + 1: ag(1, XN + 1, "x"),
        Z2: ag(ZM, Z2, "p"), Z2 + 1: ag(ZP + 1, Z2 + 1, "m"),
        ZMX[0]: ag(XN, ZMX[0], "p"), ZPX[0]: ag(XN, ZPX[0], "m"),
        ZMX[1]: ag(XN + 1, ZMX[1], "p"), ZPX[1]: ag(XN + 1, ZPX[1], "m"),
        Z2X[0]: ag(Z2, Z2X[0], "x"), Z2X[1]: ag(Z2 + 1, Z2X[1], "x"),
    }
    for slot in (ZM, ZP + 1, XN, ZM + 1, ZP, XN + 1):
        gather[slot].start()

    def tell(k, src, dst, **way):
        return to(src, dst, meta_send.at[k], meta_recv.at[k], **way)

    tell_core = [tell(0, meta.at[0, 0, 0, 0], meta.at[0, 0, 0, 1], dc=1)]
    tell_x = [tell(far, meta.at[0, 0, 0], meta.at[0, 0, far], dx=far) for far in (1, 2, 3)]
    tell_y = [tell(3 + far, meta.at[0, 0], meta.at[0, far], dy=far) for far in (1, 2, 3)]
    tell_z = [tell(6 + far, meta.at[0], meta.at[far], dz=far) for far in (1, 2, 3)]
    for copy in tell_core:
        copy.start()

    for copy in tell_core:
        copy.wait_recv()
    for copy in tell_x:
        copy.start()

    keys = []
    for chip_core in range(2):
        shard = meta[0, 0, 0, chip_core, 0:1, :]
        wide = jnp.broadcast_to(shard, (CB, CB))
        earlier = (jnp.transpose(wide) == wide) & (
            lax.broadcasted_iota(I32, (CB, CB), 0) < lax.broadcasted_iota(I32, (CB, CB), 1)
        )
        place = jnp.sum(earlier.astype(I32), axis=0, keepdims=True)
        keys.append((shard * MOST + place) * 4 + chip_core * 2)
    keys = jnp.concatenate([keys[0], keys[1], keys[0] + 1, keys[1] + 1], axis=1)

    def fill(i, _):
        row = i * 256 + lax.broadcasted_iota(I32, (256, 1), 0)
        block = row // 16
        across = (x + block % 4) % 4
        to_shard = ((z + block // 16) % 4 * 2 + across % 2) * 16 + (
            across // 2 * 8 + (y + block // 4 % 4) % 4 * 2 + core
        )
        key = (to_shard * MOST + row % 4) * 4 + row // 4 % 4
        sel[pl.ds(pl.multiple_of(i * 256, 256), 256), :] = (key == keys).astype(F32).astype(BF16)
        return 0

    lax.fori_loop(0, 16 * PAIRS // 256, fill, 0)
    q_copy.wait()
    for copy in own:
        copy.wait()

    def scores(which):
        first, number = GROUPS[which]

        def part(i, _):
            span = pl.ds(pl.multiple_of(i * 256, 256), 256)
            s = lax.dot_general(
                c[first : first + number].reshape(number * HB, D), q[span, :],
                (((1,), (1,)), ((), ())), preferred_element_type=F32,
            ) * SCALE
            top = jnp.max(s, axis=0, keepdims=True)
            shifted = jnp.exp(s - top)
            e[first : first + number, :, span] = shifted.reshape(number, HB, 256)
            mx[which : which + 1, span] = top
            sm[which : which + 1, span] = jnp.sum(shifted, axis=0, keepdims=True)
            return 0

        lax.fori_loop(0, NQ // 256, part, 0)

    def landing_rows():
        for copy in tell_z:
            copy.wait_recv()
        everyone = meta[...].reshape(SHARDS, 2, CB)
        shards, numbers = everyone[:, 0, :], everyone[:, 1, :]
        hits = (shards == blk * 16 + dp).astype(F32)
        before = (
            lax.broadcasted_iota(I32, (CB, CB), 0) < lax.broadcasted_iota(I32, (CB, CB), 1)
        ).astype(F32).astype(BF16)
        spot = jnp.dot(hits.astype(BF16), before, preferred_element_type=F32)
        numbers = (numbers + 1).astype(F32) * hits
        lanes = lax.broadcasted_iota(I32, (SHARDS, 8 * SHARDS), 1)
        spread = lanes // 8 == lax.broadcasted_iota(I32, (SHARDS, 8 * SHARDS), 0)
        spread = spread.astype(F32).astype(BF16)
        slot = lax.broadcasted_iota(I32, (8, 8 * SHARDS), 1) % 4
        key = jnp.zeros((8, 8 * SHARDS), F32)
        for k in range(MOST):
            chosen = jnp.where(spot == float(k), numbers, 0.0).astype(BF16)
            by_source = lax.dot_general(
                jnp.ones((8, CB), BF16), chosen, (((1,), (1,)), ((), ())),
                preferred_element_type=F32,
            )
            by_slot = jnp.dot(by_source.astype(BF16), spread, preferred_element_type=F32)
            key = key + jnp.where(slot == k, by_slot, 0.0)
        key = key[0:1].astype(I32) - 1
        part = lax.broadcasted_iota(I32, (1, 8 * SHARDS), 1) // 4 % 2
        for k in range(2):
            mine = jnp.where(part == k, key, -1)
            for piece in range(HR // 64):
                rows = piece * 64 + lax.broadcasted_iota(I32, (64, 8 * SHARDS), 0)
                first = k * HR + piece * 64
                land[first : first + 64, :] = (rows == mine).astype(F32).astype(BF16)

    gather[ZM].wait_recv()
    gather[Z2].start()
    gather[ZP + 1].wait_recv()
    gather[Z2 + 1].start()
    gather[XN].wait_recv()
    gather[XN + 1].wait_recv()
    scores(0)
    for copy in tell_x:
        copy.wait_recv()
    for copy in tell_y:
        copy.start()
    gather[ZM + 1].wait_recv()
    gather[ZP].wait_recv()
    scores(1)
    for copy in tell_y:
        copy.wait_recv()
    for copy in tell_z:
        copy.start()
    gather[Z2].wait_recv()
    gather[Z2X[0]].start()
    gather[Z2 + 1].wait_recv()
    gather[Z2X[1]].start()
    for slot in (ZMX[0], ZPX[0], ZMX[1], ZPX[1]):
        gather[slot].start()
    landing_rows()
    for slot in (ZPX[0], ZMX[0], Z2X[0]):
        gather[slot].wait_recv()
    scores(2)
    for slot in (ZPX[1], ZMX[1], Z2X[1]):
        gather[slot].wait_recv()
    scores(3)

    top = jnp.max(mx[0:4], axis=0, keepdims=True)
    rescale = jnp.exp(mx[0:4] - top)
    inverse = 1.0 / jnp.sum(rescale * sm[0:4], axis=0, keepdims=True)
    weight, target = w_ref[...], pos_ref[...]
    places = {
        0: at(0, 0), 2: at(0, 1), 4: at(1, 0), 6: at(3, 0), 8: at(2, 0),
    }
    starts = [0] * 16
    for first, owner in places.items():
        starts[first], starts[first + 1] = owner * CB, owner * CB + HB
    for (low, high), owner in ((ZPX, at(1, 1)), (ZMX, at(3, 1)), (Z2X, at(2, 1))):
        starts[low], starts[high] = owner * CB, owner * CB + HB
    for which, (first, number) in enumerate(GROUPS):
        factor = rescale[which : which + 1] * inverse
        for k in range(first, first + number):
            ids = starts[k] + lax.broadcasted_iota(I32, (HB, NQ), 0)
            onehot = (ids == target).astype(F32)
            coef_t[k] = (weight * (e[k] * factor - onehot)).astype(BF16)

    def message(m, chunk):
        first, number, way = MESSAGES[m]
        return pltpu.make_async_remote_copy(
            src_ref=snd.at[chunk, pl.ds(first, number)],
            dst_ref=rcv.at[chunk, pl.ds(first, number)],
            send_sem=rs_send.at[chunk, m],
            recv_sem=rs_recv.at[chunk, m],
            device_id={"blk": peers[way]},
            device_id_type=pl.DeviceIdType.MESH,
        )

    def qg_copy(chunk):
        return pltpu.make_async_copy(
            qg.at[lax.rem(chunk, 2)],
            qg_hbm.at[0, :, pl.ds(pl.multiple_of(chunk * QW, QW), QW)],
            qg_sem.at[lax.rem(chunk, 2)],
        )

    def put(chunk, slot, value):
        snd[chunk, slot] = value.astype(BF16)

    def got(chunk, slot):
        return rcv[chunk, slot].astype(F32)

    def kept(chunk, slot):
        return prod[lax.rem(chunk, 4), KEEP[slot]]

    def core_copy(k):
        return to(grad.at[k, 0], grad.at[k, 1], core_send.at[k], core_recv.at[k], dc=1)

    def dispatch(k):
        parts = []
        for chunk in range(PER):
            core_copy(k * PER + chunk).wait_recv()
        for part in range(2):
            for chip_core in range(2):
                first = part * BW
                while first < part * BW + BW:
                    width = min(BW, CW - first % CW)
                    parts.append(grad[k * PER + first // CW, chip_core, :, first % CW : first % CW + width])
                    first += width
        assert len(parts) == 4
        rows = jnp.concatenate(parts, axis=0)
        slots = jnp.dot(sel[...], rows, preferred_element_type=F32).astype(BF16)
        sent[k] = slots.reshape(PAIRS, 16, BW)
        landed[k, 0] = slots[0:16]
        for dz, dy, dx in AWAY:
            n = dz * 16 + dy * 4 + dx
            to(sent.at[k, n], landed.at[k, n], slot_send.at[k], slot_recv.at[k],
               dz=dz, dy=dy, dx=dx).start()

    def out_copy(chunk):
        return pltpu.make_async_copy(
            out.at[chunk],
            out_hbm.at[:, pl.ds(pl.multiple_of(chunk * 2 * BW, 2 * BW), 2 * BW)],
            out_sem.at[chunk],
        )

    def touch_down(k):
        whole(landed.at[k, pl.ds(1, PAIRS - 1)], slot_recv.at[k])
        total = jnp.dot(
            land[...], landed[k].reshape(16 * PAIRS, BW), preferred_element_type=F32
        )
        for part in range(2):
            out[k, :, part * BW : part * BW + BW] = total[part * HR : part * HR + HR]
        out_copy(k).start()

    def step(i, _):
        @pl.when(i < NC)
        def _():
            slab = lax.rem(i, 4)
            columns = pl.ds(pl.multiple_of(i * CW, CW), CW)
            block = jnp.dot(
                coef_t[...].reshape(16 * HB, NQ), q[:, columns], preferred_element_type=F32
            ) * SCALE
            block = block.reshape(16, HB, CW)
            for slot, k in KEEP.items():
                prod[slab, k] = block[slot]
            for k, slot in enumerate(Z2X + ZPX + ZMX + (ZP, ZM + 1)):
                put(i, k, block[slot])
            for m in range(5):
                message(m, i).start()

        @pl.when((i >= 1) & (i <= NC))
        def _():
            k = i - 1
            message(0, k).wait_recv()
            put(k, 9, kept(k, Z2) + got(k, 0))
            message(6, k).start()
            put(k, 8, kept(k, Z2 + 1) + got(k, 1))
            message(5, k).start()
            message(1, k).wait_recv()
            message(2, k).wait_recv()
            put(k, 10, kept(k, XN) + got(k, 2) + got(k, 4))
            put(k, 11, kept(k, XN + 1) + got(k, 3) + got(k, 5))
            message(7, k).start()

        @pl.when((i >= 2) & (i <= NC + 1))
        def _():
            k = i - 2
            message(5, k).wait_recv()
            put(k, 12, kept(k, ZP + 1) + got(k, 8))
            message(8, k).start()
            message(6, k).wait_recv()
            put(k, 13, kept(k, ZM) + got(k, 9))
            message(9, k).start()

        @pl.when((i >= 3) & (i <= NC + 2))
        def _():
            k = i - 3
            for m in (3, 4, 7, 8, 9):
                message(m, k).wait_recv()
            low = kept(k, SELF) + got(k, 6) + got(k, 13) + got(k, 10)
            high = kept(k, SELF + 1) + got(k, 7) + got(k, 12) + got(k, 11)
            grad[k, 0, 0:HB] = low.astype(BF16)
            grad[k, 0, HB:CB] = high.astype(BF16)
            core_copy(k).start()

        @pl.when((i >= 3 + PER) & (lax.rem(i - 3, PER) == 0))
        def _():
            dispatch(lax.div(i - 3, PER) - 1)

        @pl.when(i == NC - 1)
        def _():
            for k in range(4):
                coef[pl.ds(k * 256, 256), :] = jnp.transpose(
                    coef_t[:, :, k * 256 : k * 256 + 256].reshape(16 * HB, 256)
                )

        @pl.when(i >= NC - 1)
        def _():
            query_part(i - (NC - 1))

        return 0

    def query_part(k):
        @pl.when(k >= 2)
        def _():
            qg_copy(k - 2).wait()

        for half in range(QW // 256):
            columns = pl.ds(pl.multiple_of(k * QW + half * 256, 256), 256)
            total = jnp.dot(
                coef[...], c[:, :, columns].reshape(16 * HB, 256), preferred_element_type=F32
            )
            qg[lax.rem(k, 2), :, half * 256 : half * 256 + 256] = (total * SCALE).astype(BF16)
        qg_copy(k).start()

    lax.fori_loop(0, NC + 4, step, 0)

    def land_part(k, _):
        touch_down(k)
        return 0

    lax.fori_loop(0, ND, land_part, 0)

    for copy in gather.values():
        copy.wait_send()

    for copy in tell_core + tell_x + tell_y + tell_z:
        copy.wait_send()

    def drain(i, _):
        for m in range(NM):
            message(m, i).wait_send()
        core_copy(i).wait_send()
        return 0

    lax.fori_loop(0, NC, drain, 0)
    for k in range(ND):
        whole(sent.at[k, pl.ds(1, PAIRS - 1)], slot_send.at[k])
        out_copy(k).wait()
    qg_copy(D // QW - 2).wait()
    qg_copy(D // QW - 1).wait()


def per_device(queries, candidates, loss_weight, positives, producers, rows):
    vmem, hbm = pl.BlockSpec(memory_space=pltpu.VMEM), pl.BlockSpec(memory_space=pl.ANY)
    shard_row = producers.reshape(1, CB)
    return pl.pallas_call(
        main_kernel,
        out_shape=(
            jax.ShapeDtypeStruct((1, NQ, D), BF16),
            jax.ShapeDtypeStruct((HR, D), F32),
        ),
        in_specs=[hbm, hbm, vmem, vmem, vmem, vmem],
        out_specs=(hbm, hbm),
        scratch_shapes=[
            pltpu.VMEM((NQ, D), BF16),
            pltpu.VMEM((16, HB, D), BF16),
            pltpu.VMEM((16, HB, NQ), F32),
            pltpu.VMEM((16, HB, NQ), BF16),
            pltpu.VMEM((NQ, 16 * HB), BF16),
            pltpu.VMEM((4, len(KEEP), HB, CW), F32),
            pltpu.VMEM((NC, 14, HB, CW), BF16),
            pltpu.VMEM((NC, 14, HB, CW), BF16),
            pltpu.VMEM((2, NQ, QW), BF16),
            pltpu.VMEM((16 * PAIRS, 4 * CB), BF16),
            pltpu.VMEM((8, NQ), F32),
            pltpu.VMEM((8, NQ), F32),
            pltpu.VMEM((4, 4, 4, 2, 2, CB), I32),
            pltpu.VMEM((2 * HR, 8 * SHARDS), BF16),
            pltpu.VMEM((ND, HR, 2 * BW), F32),
            pltpu.VMEM((NC, 2, CB, CW), BF16),
            pltpu.VMEM((ND, PAIRS, 16, BW), BF16),
            pltpu.VMEM((ND, PAIRS, 16, BW), BF16),
            pltpu.SemaphoreType.DMA,
            pltpu.SemaphoreType.DMA((2,)),
            pltpu.SemaphoreType.DMA((16,)),
            pltpu.SemaphoreType.DMA((16,)),
            pltpu.SemaphoreType.DMA((NC, NM)),
            pltpu.SemaphoreType.DMA((NC, NM)),
            pltpu.SemaphoreType.DMA((2,)),
            pltpu.SemaphoreType.DMA((ND,)),
            pltpu.SemaphoreType.DMA((10,)),
            pltpu.SemaphoreType.DMA((10,)),
            pltpu.SemaphoreType.DMA((NC,)),
            pltpu.SemaphoreType.DMA((NC,)),
            pltpu.SemaphoreType.DMA((ND,)),
            pltpu.SemaphoreType.DMA((ND,)),
        ],
        compiler_params=pltpu.CompilerParams(
            collective_id=0, has_side_effects=True, vmem_limit_bytes=62 * 2**20
        ),
        cost_estimate=pl.CostEstimate(
            flops=6 * NQ * NQ * D, bytes_accessed=20 * 2**20, transcendentals=NQ * NQ
        ),
        name="listwise_backward",
    )(queries, candidates, loss_weight, positives, shard_row, rows)


def solution(mesh):
    return jax.shard_map(
        per_device,
        mesh=mesh,
        in_specs=(
            P("dp", "blk", None),
            P("dp", "blk", None),
            P("dp", "blk"),
            P("dp", "blk"),
            P("dp", "blk", None),
            P("dp", "blk"),
        ),
        out_specs=(P("dp", "blk", None), P(("blk", "dp"), None)),
        check_vma=False,
    )
```

time: 137 us -> 134 us (0.978)
  Pallas kernels: 130 us -> 127 us
    pallas_call x1, Pallas kernels: 130 us -> 127 us  [per_device(): pl.pallas_call(main_kernel, out_shape=(jax.ShapeDtypeStruct((1, NQ, D), B...]
where the time goes in v4:
time: 134 us
  Pallas kernels  127 us (95%)
  local copies, waits for them, and re-layouts  6.83 us (5%)
    pallas_call x1, Pallas kernels, per_device(): pl.pallas_call(main_kernel, out_shape=(jax.ShapeDtypeStruct((1, NQ, D), B...  127 us
    unnamed x4, local copies, waits for them, and re-layouts  6.83 us

profile of v4, /device:TPU:0, one launch (start us, length us, event | category | flops | bytes accessed | tf_op | source)
XLA Modules:
  0.0 134.2 jit_solution(451745302525271939)
XLA Ops:
  0.6 126.7 %listwise_backward.1 = (bf16[1,1024,2560]{2,1,0:T(8,128)(2,1)}, f32[256,2560]{1,0:T(8,128)}) custom-call(bf16[1,1024,2560]{2,1,0:T(8,128)(2,1)} %q_hbm.1, bf16[1,128,2560]{2,1,0:T(8,128)(2,1)} %c_hbm.1, f32[1,1024]{1,0:T(1,128)} %w_ref.1, s32[1,1024]{1,0:T(1,128)} %pos_ref.1, s32[1,128]{1,0:T(1,128)} %bitcast.1, s32[1,128]{1,0:T(1,128)} %row_ref.1), custom_call_target="tpu_custom_call" | custom-call | flops 16106127360 | bytes 20971520 | tf_op jit(solution)/shard_map/listwise_backward/pallas_call | solution.py:441
  127.3 0.0 copy-start
  127.4 5.3 %copy.10 = bf16[1,1024,2560]{2,1,0:T(8,128)(2,1)} copy(bf16[1,1024,2560]{2,1,0:T(8,128)(2,1)} %get-tuple-element.4) | data formatting | bytes 10485760
  132.7 0.0 copy-done
  132.7 1.5 %copy.11 = f32[256,2560]{1,0:T(8,128)} copy(f32[256,2560]{1,0:T(8,128)S(1)} %copy-done) | data formatting | bytes 5242880
Async XLA Ops:
  127.3 5.3 %copy-start = (f32[256,2560]{1,0:T(8,128)S(1)}, f32[256,2560]{1,0:T(8,128)}, u32[]{:S(2)}) copy-start(f32[256,2560]{1,0:T(8,128)} %get-tuple-element.5) | copy-start | bytes 7864324

commit v5 on v4

--- a/solution.py
+++ b/solution.py
@@ -14,6 +14,7 @@
 NQ = 1024
 CB = 128
 HB = 64
+STAY = 48
 NC = 5
 CW = D // NC
 ND = 5
@@ -29,8 +30,9 @@
 GROUPS = ((0, 4), (4, 4), (8, 5), (13, 3))
 
 MESSAGES = (
-    (0, 2, "x"), (2, 2, "p"), (4, 2, "m"), (6, 1, "p"), (7, 1, "m"),
-    (8, 1, "p"), (9, 1, "m"), (10, 2, "x"), (12, 1, "p"), (13, 1, "m"),
+    (0, 128, "x"), (128, 64 + STAY, "p"), (256, 64 + STAY, "m"), (384, 64, "p"), (448, 64, "m"),
+    (512, 64, "p"), (576, 64, "m"), (640, 128, "x"), (768, 64, "p"), (832, 64, "m"),
+    (192 + STAY, 64 - STAY, "x"), (320 + STAY, 64 - STAY, "x"),
 )
 NM = len(MESSAGES)
 KEEP = {SELF: 0, SELF + 1: 1, XN: 2, XN + 1: 3, ZP: 4, ZP + 1: 5, ZM: 6, ZM + 1: 7, Z2: 8, Z2 + 1: 9}
@@ -93,13 +95,17 @@
         )
     pl.semaphore_wait(barrier, len(lines))
 
-    def ag(src, dst, way):
-        source = c_hbm.at[0, pl.ds(src * HB, HB)] if src < 2 else c.at[src]
+    def ag(src, dst, way, first=0, number=HB, sem=None):
+        if src < 2:
+            source = c_hbm.at[0, pl.ds(src * HB + first, number)]
+        else:
+            source = c.at[src, pl.ds(first, number)]
+        sem = dst if sem is None else sem
         return pltpu.make_async_remote_copy(
             src_ref=source,
-            dst_ref=c.at[dst],
-            send_sem=ag_send.at[dst],
-            recv_sem=ag_recv.at[dst],
+            dst_ref=c.at[dst, pl.ds(first, number)],
+            send_sem=ag_send.at[sem],
+            recv_sem=ag_recv.at[sem],
             device_id={"blk": peers[way]},
             device_id_type=pl.DeviceIdType.MESH,
         )
@@ -109,7 +115,9 @@
         ZM + 1: ag(1, ZM + 1, "p"), ZP: ag(0, ZP, "m"), XN + 1: ag(1, XN + 1, "x"),
         Z2: ag(ZM, Z2, "p"), Z2 + 1: ag(ZP + 1, Z2 + 1, "m"),
         ZMX[0]: ag(XN, ZMX[0], "p"), ZPX[0]: ag(XN, ZPX[0], "m"),
-        ZMX[1]: ag(XN + 1, ZMX[1], "p"), ZPX[1]: ag(XN + 1, ZPX[1], "m"),
+        ZMX[1]: ag(XN + 1, ZMX[1], "p", 0, STAY), ZPX[1]: ag(XN + 1, ZPX[1], "m", 0, STAY),
+        16: ag(ZM + 1, ZMX[1], "x", STAY, HB - STAY, 16),
+        17: ag(ZP + 1, ZPX[1], "x", STAY, HB - STAY, 17),
         Z2X[0]: ag(Z2, Z2X[0], "x"), Z2X[1]: ag(Z2 + 1, Z2X[1], "x"),
     }
     for slot in (ZM, ZP + 1, XN, ZM + 1, ZP, XN + 1):
@@ -219,7 +227,9 @@
         copy.wait_recv()
     for copy in tell_y:
         copy.start()
+    gather[17].start()
     gather[ZM + 1].wait_recv()
+    gather[16].start()
     gather[ZP].wait_recv()
     scores(1)
     for copy in tell_y:
@@ -236,7 +246,7 @@
     for slot in (ZPX[0], ZMX[0], Z2X[0]):
         gather[slot].wait_recv()
     scores(2)
-    for slot in (ZPX[1], ZMX[1], Z2X[1]):
+    for slot in (ZPX[1], ZMX[1], 16, 17, Z2X[1]):
         gather[slot].wait_recv()
     scores(3)
 
@@ -278,10 +288,16 @@
         )
 
     def put(chunk, slot, value):
-        snd[chunk, slot] = value.astype(BF16)
+        snd[chunk, slot * HB : slot * HB + HB] = value.astype(BF16)
 
     def got(chunk, slot):
-        return rcv[chunk, slot].astype(F32)
+        return rcv[chunk, slot * HB : slot * HB + HB].astype(F32)
+
+    def by_z(chunk, slot):
+        return jnp.where(lax.broadcasted_iota(I32, (HB, CW), 0) < STAY, got(chunk, slot), 0.0)
+
+    def by_x(chunk, slot):
+        return jnp.where(lax.broadcasted_iota(I32, (HB, CW), 0) >= STAY, got(chunk, slot), 0.0)
 
     def kept(chunk, slot):
         return prod[lax.rem(chunk, 4), KEEP[slot]]
@@ -331,15 +347,24 @@
         def _():
             slab = lax.rem(i, 4)
             columns = pl.ds(pl.multiple_of(i * CW, CW), CW)
-            block = jnp.dot(
-                coef_t[...].reshape(16 * HB, NQ), q[:, columns], preferred_element_type=F32
-            ) * SCALE
-            block = block.reshape(16, HB, CW)
+            def product(first, number):
+                block = jnp.dot(
+                    coef_t[first : first + number].reshape(number * HB, NQ), q[:, columns],
+                    preferred_element_type=F32,
+                ) * SCALE
+                return block.reshape(number, HB, CW)
+
+            block = product(10, 6)
+            for k, slot in enumerate(Z2X + ZPX + ZMX[::-1]):
+                put(i, k, block[slot - 10])
+            for m in (0, 1, 2, 10, 11):
+                message(m, i).start()
+            block = product(0, 10)
             for slot, k in KEEP.items():
                 prod[slab, k] = block[slot]
-            for k, slot in enumerate(Z2X + ZPX + ZMX + (ZP, ZM + 1)):
-                put(i, k, block[slot])
-            for m in range(5):
+            put(i, 6, block[ZP])
+            put(i, 7, block[ZM + 1])
+            for m in (3, 4):
                 message(m, i).start()
 
         @pl.when((i >= 1) & (i <= NC))
@@ -350,20 +375,20 @@
             message(6, k).start()
             put(k, 8, kept(k, Z2 + 1) + got(k, 1))
             message(5, k).start()
-            message(1, k).wait_recv()
-            message(2, k).wait_recv()
-            put(k, 10, kept(k, XN) + got(k, 2) + got(k, 4))
-            put(k, 11, kept(k, XN + 1) + got(k, 3) + got(k, 5))
+            for m in (1, 2, 10, 11):
+                message(m, k).wait_recv()
+            put(k, 10, kept(k, XN) + got(k, 2) + by_z(k, 5))
+            put(k, 11, kept(k, XN + 1) + by_z(k, 3) + got(k, 4))
             message(7, k).start()
 
         @pl.when((i >= 2) & (i <= NC + 1))
         def _():
             k = i - 2
             message(5, k).wait_recv()
-            put(k, 12, kept(k, ZP + 1) + got(k, 8))
+            put(k, 12, kept(k, ZP + 1) + got(k, 8) + by_x(k, 3))
             message(8, k).start()
             message(6, k).wait_recv()
-            put(k, 13, kept(k, ZM) + got(k, 9))
+            put(k, 13, kept(k, ZM) + got(k, 9) + by_x(k, 5))
             message(9, k).start()
 
         @pl.when((i >= 3) & (i <= NC + 2))
@@ -453,8 +478,8 @@
             pltpu.VMEM((16, HB, NQ), BF16),
             pltpu.VMEM((NQ, 16 * HB), BF16),
             pltpu.VMEM((4, len(KEEP), HB, CW), F32),
-            pltpu.VMEM((NC, 14, HB, CW), BF16),
-            pltpu.VMEM((NC, 14, HB, CW), BF16),
+            pltpu.VMEM((NC, 14 * HB, CW), BF16),
+            pltpu.VMEM((NC, 14 * HB, CW), BF16),
             pltpu.VMEM((2, NQ, QW), BF16),
             pltpu.VMEM((16 * PAIRS, 4 * CB), BF16),
             pltpu.VMEM((8, NQ), F32),
@@ -467,8 +492,8 @@
             pltpu.VMEM((ND, PAIRS, 16, BW), BF16),
             pltpu.SemaphoreType.DMA,
             pltpu.SemaphoreType.DMA((2,)),
-            pltpu.SemaphoreType.DMA((16,)),
-            pltpu.SemaphoreType.DMA((16,)),
+            pltpu.SemaphoreType.DMA((18,)),
+            pltpu.SemaphoreType.DMA((18,)),
             pltpu.SemaphoreType.DMA((NC, NM)),
             pltpu.SemaphoreType.DMA((NC, NM)),
             pltpu.SemaphoreType.DMA((2,)),

time: 134 us -> 130 us (0.970)
  Pallas kernels: 127 us -> 122 us
    pallas_call x1, Pallas kernels: 127 us -> 122 us  [per_device(): pl.pallas_call(main_kernel, out_shape=(jax.ShapeDtypeStruct((1, NQ, D), B...]
where the time goes in v5:
time: 130 us
  Pallas kernels  122 us (94%)
  local copies, waits for them, and re-layouts  6.83 us (5%)
    pallas_call x1, Pallas kernels, per_device(): pl.pallas_call(main_kernel, out_shape=(jax.ShapeDtypeStruct((1, NQ, D), B...  122 us
    unnamed x4, local copies, waits for them, and re-layouts  6.83 us

profile of v5, /device:TPU:0, one launch (start us, length us, event | category | flops | bytes accessed | tf_op | source)
XLA Modules:
  0.0 129.8 jit_solution(4754321583767048058)
XLA Ops:
  0.6 122.3 %listwise_backward.1 = (bf16[1,1024,2560]{2,1,0:T(8,128)(2,1)}, f32[256,2560]{1,0:T(8,128)}) custom-call(bf16[1,1024,2560]{2,1,0:T(8,128)(2,1)} %q_hbm.1, bf16[1,128,2560]{2,1,0:T(8,128)(2,1)} %c_hbm.1, f32[1,1024]{1,0:T(1,128)} %w_ref.1, s32[1,1024]{1,0:T(1,128)} %pos_ref.1, s32[1,128]{1,0:T(1,128)} %bitcast.1, s32[1,128]{1,0:T(1,128)} %row_ref.1), custom_call_target="tpu_custom_call" | custom-call | flops 16106127360 | bytes 20971520 | tf_op jit(solution)/shard_map/listwise_backward/pallas_call | solution.py:466
  123.0 0.0 copy-start
  123.0 5.3 %copy.10 = bf16[1,1024,2560]{2,1,0:T(8,128)(2,1)} copy(bf16[1,1024,2560]{2,1,0:T(8,128)(2,1)} %get-tuple-element.4) | data formatting | bytes 10485760
  128.3 0.0 copy-done
  128.3 1.5 %copy.11 = f32[256,2560]{1,0:T(8,128)} copy(f32[256,2560]{1,0:T(8,128)S(1)} %copy-done) | data formatting | bytes 5242880
Async XLA Ops:
  123.0 5.3 %copy-start = (f32[256,2560]{1,0:T(8,128)S(1)}, f32[256,2560]{1,0:T(8,128)}, u32[]{:S(2)}) copy-start(f32[256,2560]{1,0:T(8,128)} %get-tuple-element.5) | copy-start | bytes 7864324

commit v6 on v5

--- a/solution.py
+++ b/solution.py
@@ -14,7 +14,7 @@
 NQ = 1024
 CB = 128
 HB = 64
-STAY = 48
+STAY = 32
 NC = 5
 CW = D // NC
 ND = 5

time: 130 us -> 128 us (0.985)
  Pallas kernels: 122 us -> 120 us
    pallas_call x1, Pallas kernels: 122 us -> 120 us  [per_device(): pl.pallas_call(main_kernel, out_shape=(jax.ShapeDtypeStruct((1, NQ, D), B...]
where the time goes in v6:
time: 128 us
  Pallas kernels  120 us (94%)
  local copies, waits for them, and re-layouts  6.83 us (5%)
    pallas_call x1, Pallas kernels, per_device(): pl.pallas_call(main_kernel, out_shape=(jax.ShapeDtypeStruct((1, NQ, D), B...  120 us
    unnamed x4, local copies, waits for them, and re-layouts  6.83 us

profile of v6, /device:TPU:0, one launch (start us, length us, event | category | flops | bytes accessed | tf_op | source)
XLA Modules:
  0.0 128.0 jit_solution(18012966914320630269)
XLA Ops:
  0.6 120.5 %listwise_backward.1 = (bf16[1,1024,2560]{2,1,0:T(8,128)(2,1)}, f32[256,2560]{1,0:T(8,128)}) custom-call(bf16[1,1024,2560]{2,1,0:T(8,128)(2,1)} %q_hbm.1, bf16[1,128,2560]{2,1,0:T(8,128)(2,1)} %c_hbm.1, f32[1,1024]{1,0:T(1,128)} %w_ref.1, s32[1,1024]{1,0:T(1,128)} %pos_ref.1, s32[1,128]{1,0:T(1,128)} %bitcast.1, s32[1,128]{1,0:T(1,128)} %row_ref.1), custom_call_target="tpu_custom_call" | custom-call | flops 16106127360 | bytes 20971520 | tf_op jit(solution)/shard_map/listwise_backward/pallas_call | solution.py:466
  121.1 0.0 copy-start
  121.1 5.3 %copy.10 = bf16[1,1024,2560]{2,1,0:T(8,128)(2,1)} copy(bf16[1,1024,2560]{2,1,0:T(8,128)(2,1)} %get-tuple-element.4) | data formatting | bytes 10485760
  126.5 0.0 copy-done
  126.5 1.5 %copy.11 = f32[256,2560]{1,0:T(8,128)} copy(f32[256,2560]{1,0:T(8,128)S(1)} %copy-done) | data formatting | bytes 5242880
Async XLA Ops:
  121.1 5.3 %copy-start = (f32[256,2560]{1,0:T(8,128)S(1)}, f32[256,2560]{1,0:T(8,128)}, u32[]{:S(2)}) copy-start(f32[256,2560]{1,0:T(8,128)} %get-tuple-element.5) | copy-start | bytes 7864324

commit v7 on v6

--- a/solution.py
+++ b/solution.py
@@ -14,6 +14,7 @@
 NQ = 1024
 CB = 128
 HB = 64
+KEEP_G = 48
 STAY = 32
 NC = 5
 CW = D // NC
@@ -115,9 +116,9 @@
         ZM + 1: ag(1, ZM + 1, "p"), ZP: ag(0, ZP, "m"), XN + 1: ag(1, XN + 1, "x"),
         Z2: ag(ZM, Z2, "p"), Z2 + 1: ag(ZP + 1, Z2 + 1, "m"),
         ZMX[0]: ag(XN, ZMX[0], "p"), ZPX[0]: ag(XN, ZPX[0], "m"),
-        ZMX[1]: ag(XN + 1, ZMX[1], "p", 0, STAY), ZPX[1]: ag(XN + 1, ZPX[1], "m", 0, STAY),
-        16: ag(ZM + 1, ZMX[1], "x", STAY, HB - STAY, 16),
-        17: ag(ZP + 1, ZPX[1], "x", STAY, HB - STAY, 17),
+        ZMX[1]: ag(XN + 1, ZMX[1], "p", 0, KEEP_G), ZPX[1]: ag(XN + 1, ZPX[1], "m", 0, KEEP_G),
+        16: ag(ZM + 1, ZMX[1], "x", KEEP_G, HB - KEEP_G, 16),
+        17: ag(ZP + 1, ZPX[1], "x", KEEP_G, HB - KEEP_G, 17),
         Z2X[0]: ag(Z2, Z2X[0], "x"), Z2X[1]: ag(Z2 + 1, Z2X[1], "x"),
     }
     for slot in (ZM, ZP + 1, XN, ZM + 1, ZP, XN + 1):

time: 128 us -> 126 us (0.984)
  Pallas kernels: 120 us -> 118 us
    pallas_call x1, Pallas kernels: 120 us -> 118 us  [per_device(): pl.pallas_call(main_kernel, out_shape=(jax.ShapeDtypeStruct((1, NQ, D), B...]
where the time goes in v7:
time: 126 us
  Pallas kernels  118 us (94%)
  local copies, waits for them, and re-layouts  6.83 us (5%)
    pallas_call x1, Pallas kernels, per_device(): pl.pallas_call(main_kernel, out_shape=(jax.ShapeDtypeStruct((1, NQ, D), B...  118 us
    unnamed x4, local copies, waits for them, and re-layouts  6.83 us

profile of v7, /device:TPU:0, one launch (start us, length us, event | category | flops | bytes accessed | tf_op | source)
XLA Modules:
  0.0 125.8 jit_solution(6930899524895771483)
XLA Ops:
  0.6 118.3 %listwise_backward.1 = (bf16[1,1024,2560]{2,1,0:T(8,128)(2,1)}, f32[256,2560]{1,0:T(8,128)}) custom-call(bf16[1,1024,2560]{2,1,0:T(8,128)(2,1)} %q_hbm.1, bf16[1,128,2560]{2,1,0:T(8,128)(2,1)} %c_hbm.1, f32[1,1024]{1,0:T(1,128)} %w_ref.1, s32[1,1024]{1,0:T(1,128)} %pos_ref.1, s32[1,128]{1,0:T(1,128)} %bitcast.1, s32[1,128]{1,0:T(1,128)} %row_ref.1), custom_call_target="tpu_custom_call" | custom-call | flops 16106127360 | bytes 20971520 | tf_op jit(solution)/shard_map/listwise_backward/pallas_call | solution.py:467
  118.9 0.0 copy-start
  118.9 5.3 %copy.10 = bf16[1,1024,2560]{2,1,0:T(8,128)(2,1)} copy(bf16[1,1024,2560]{2,1,0:T(8,128)(2,1)} %get-tuple-element.4) | data formatting | bytes 10485760
  124.3 0.0 copy-done
  124.3 1.5 %copy.11 = f32[256,2560]{1,0:T(8,128)} copy(f32[256,2560]{1,0:T(8,128)S(1)} %copy-done) | data formatting | bytes 5242880
Async XLA Ops:
  118.9 5.3 %copy-start = (f32[256,2560]{1,0:T(8,128)S(1)}, f32[256,2560]{1,0:T(8,128)}, u32[]{:S(2)}) copy-start(f32[256,2560]{1,0:T(8,128)} %get-tuple-element.5) | copy-start | bytes 7864324
